TPU v7x, 256 devices: a whole 4x4x8 slice. The times are simulated.
256 devices in a mesh: dp: 4 (over y), pipe: 4 (over x), expert: 16 (over z, core).
Axes of the slice: x: 4, y: 4, z: 8, core: 2. Of those that a mesh axis runs over, the one named last changes fastest.
Arguments:
- embedded: bfloat16 [3, 512, 2048], P(None, ('dp', 'expert')), may hold values from -6 to 6
- out_grad: bfloat16 [3, 512, 2048], P(None, ('dp', 'expert')), may hold values from -6 to 6
- norm_gain: float32 [4, 2048], P('pipe'), may hold values from 0.1 to 1.9
- router_weight: bfloat16 [4, 2048, 16], P('pipe'), may hold values from -0.5 to 0.5
- gate_weight: bfloat16 [4, 16, 2048, 768], P('pipe', 'expert'), may hold values from -0.125 to 0.125
- up_weight: bfloat16 [4, 16, 2048, 768], P('pipe', 'expert'), may hold values from -0.125 to 0.125
- down_weight: bfloat16 [4, 16, 768, 2048], P('pipe', 'expert'), may hold values from -0.21875 to 0.21875
- routing: int32 [4, 3, 512, 8], P('pipe', None, ('dp', 'expert')), may hold values from 0 to 15, all different within a row; in each aligned block of 8 rows (0 to 7, 8 to 15, ..., all dimensions but the last counted through in order) at most 8 rows name the same one
Outputs:
- activations: bfloat16 [4, 3, 512, 2048], P('pipe', None, ('dp', 'expert'))
- input_grads: bfloat16 [4, 3, 512, 2048], P('pipe', None, ('dp', 'expert'))
- gate_grad: bfloat16 [4, 16, 2048, 768], P('pipe', 'expert', 'dp')
- up_grad: bfloat16 [4, 16, 2048, 768], P('pipe', 'expert', 'dp')
- down_grad: bfloat16 [4, 16, 768, 2048], P('pipe', 'expert', None, 'dp')
- router_grad: float32 [4, 2048, 16], P('pipe', ('dp', 'expert'))
- gain_grad: float32 [4, 2048], P('pipe', ('dp', 'expert'))
Inputs may be any that keep to these rules, and one draw needn't show every extreme that they name: `routing`: each row names 8 different experts. In each aligned block of 8 rows (one device's tokens of one micro-batch of one layer) no expert is named by more than 8 rows; in some blocks one expert is named by exactly 8.
All inputs are finite; a program needn't handle non-finite values.
Results may differ from a plain program's by a relative error of at most 0.034.
Values may be sent and summed in bfloat16 or wider, within the bound.
A program may use at most 128 MiB of HBM per device.

v0:
```python
import jax
import jax.numpy as jnp
from jax import lax
from jax.sharding import PartitionSpec as P

CAP = 8


BEST = lax.Precision.HIGHEST
EPSILON = 1e-06


def from_behind(value, axis, steps):
    count = lax.axis_size(axis)
    first, last = (max(0, -steps), min(count, count - steps))
    return lax.ppermute(value, axis, [(source, source + steps) for source in range(first, last)])


def normalize(layer_input, gain_row):
    wide_input = layer_input.astype(jnp.float32)
    inv_rms = lax.rsqrt(jnp.mean(wide_input * wide_input, axis=-1, keepdims=True) + EPSILON)
    return ((wide_input * inv_rms * gain_row).astype(jnp.bfloat16), wide_input, inv_rms)


def slot_table(ids, expert_count):
    token_count, top_count = ids.shape
    flat_ids = ids.reshape(token_count * top_count)
    member = (flat_ids[:, None] == jnp.arange(expert_count, dtype=jnp.int32)[None, :]).astype(
        jnp.int32
    )
    earlier = jnp.cumsum(member, axis=0) - member
    slot_place = flat_ids * CAP + jnp.sum(earlier * member, axis=1)
    onehot = (
        slot_place[:, None] == jnp.arange(expert_count * CAP, dtype=jnp.int32)[None, :]
    ).astype(jnp.float32)
    return onehot.reshape(token_count, top_count, expert_count * CAP)


def token_plan(normed, router_map, ids):
    expert_count = router_map.shape[1]
    logits = jnp.dot(normed, router_map, preferred_element_type=jnp.float32)
    probs = jax.nn.sigmoid(logits)
    pick_table = (ids[..., None] == jnp.arange(expert_count, dtype=jnp.int32)).astype(jnp.float32)
    chosen = jnp.sum(pick_table * probs[..., None, :], axis=-1)
    prob_total = jnp.sum(chosen, axis=-1, keepdims=True)
    weights = chosen / prob_total
    onehot = slot_table(ids, expert_count)
    spread = jnp.sum(onehot, axis=1)
    combine = jnp.sum(onehot * weights[..., None], axis=1)
    return (weights, chosen, prob_total, pick_table, onehot, spread, combine)


def pick_micro(stored, position):
    return lax.dynamic_index_in_dim(stored, position, 0, keepdims=False)


def store_micro(stored, position, fresh, is_valid):
    previous = lax.dynamic_index_in_dim(stored, position, 0, keepdims=False)
    return lax.dynamic_update_index_in_dim(
        stored, jnp.where(is_valid, fresh, previous), position, 0
    )


def expert_forward(row_block, gate_map, up_map, down_map):
    gate_pre = jnp.dot(row_block, gate_map, preferred_element_type=jnp.float32)
    up_pre = jnp.dot(row_block, up_map, preferred_element_type=jnp.float32)
    hidden = (jax.nn.silu(gate_pre) * up_pre).astype(jnp.bfloat16)
    expert_out = jnp.dot(hidden, down_map, preferred_element_type=jnp.float32).astype(jnp.bfloat16)
    return (expert_out, gate_pre, up_pre, hidden)


def spare_forward(slot_count, model_width, hidden_units):
    return (
        jnp.zeros((slot_count, model_width), jnp.bfloat16),
        jnp.zeros((slot_count, hidden_units), jnp.float32),
        jnp.zeros((slot_count, hidden_units), jnp.float32),
        jnp.zeros((slot_count, hidden_units), jnp.bfloat16),
    )


def expert_backward(rows_grad, gate_pre, up_pre, gate_map, up_map, down_map):
    dhidden = jnp.einsum("rd,fd->rf", rows_grad, down_map, preferred_element_type=jnp.float32)
    sigma_gate = jax.nn.sigmoid(gate_pre)
    activated = gate_pre * sigma_gate
    dgate = (dhidden * up_pre * sigma_gate * (1.0 + gate_pre * (1.0 - sigma_gate))).astype(
        jnp.bfloat16
    )
    dup = (dhidden * activated).astype(jnp.bfloat16)
    drows = (
        jnp.einsum("rf,df->rd", dgate, gate_map, preferred_element_type=jnp.float32)
        + jnp.einsum("rf,df->rd", dup, up_map, preferred_element_type=jnp.float32)
    ).astype(jnp.bfloat16)
    return (drows, dgate, dup)


def spare_backward(slot_count, model_width, hidden_units):
    return (
        jnp.zeros((slot_count, model_width), jnp.bfloat16),
        jnp.zeros((slot_count, hidden_units), jnp.bfloat16),
        jnp.zeros((slot_count, hidden_units), jnp.bfloat16),
    )


def weight_terms(row_block, rows_grad, hidden, dgate, dup):
    return (
        jnp.einsum("rd,rf->df", row_block, dgate, preferred_element_type=jnp.float32),
        jnp.einsum("rd,rf->df", row_block, dup, preferred_element_type=jnp.float32),
        jnp.einsum("rd,rf->df", rows_grad, hidden, preferred_element_type=jnp.float32),
    )


def local(
    embedded, out_grad, norm_gain, router_weight, gate_weight, up_weight, down_weight, routing
):
    my_section = lax.axis_index("pipe")
    section_count = lax.axis_size("pipe")
    micro_count, token_count, model_width = embedded.shape
    gain_row = norm_gain[0]
    router_map = router_weight[0]
    expert_count = router_map.shape[1]
    gate_map = gate_weight[0, 0]
    up_map = up_weight[0, 0]
    down_map = down_weight[0, 0]
    hidden_units = gate_map.shape[1]
    slot_count = expert_count * CAP
    tick_count = micro_count + section_count - 1
    stash_input = jnp.zeros((micro_count, token_count, model_width), jnp.bfloat16)
    stash_rows = jnp.zeros((micro_count, slot_count, model_width), jnp.bfloat16)
    stash_gate = jnp.zeros((micro_count, slot_count, hidden_units), jnp.float32)
    stash_up = jnp.zeros((micro_count, slot_count, hidden_units), jnp.float32)
    stash_hidden = jnp.zeros((micro_count, slot_count, hidden_units), jnp.bfloat16)
    stash_back = jnp.zeros((micro_count, slot_count, model_width), jnp.bfloat16)
    activations = jnp.zeros((micro_count, token_count, model_width), jnp.bfloat16)
    passed = jnp.zeros((token_count, model_width), jnp.bfloat16)
    for moment in range(tick_count):
        if moment > 0:
            arrived = from_behind(passed, "pipe", 1)
        else:
            arrived = passed
        micro_index = moment - my_section
        is_valid = (micro_index >= 0) & (micro_index < micro_count)
        position = jnp.clip(micro_index, 0, micro_count - 1)
        layer_input = jnp.where(my_section == 0, pick_micro(embedded, position), arrived)
        micro_ids = pick_micro(routing[0], position)
        normed, wide_input, inv_rms = normalize(layer_input, gain_row)
        routing_plan = token_plan(normed, router_map, micro_ids)
        spread = routing_plan[5]
        combine = routing_plan[6]
        outgoing = jnp.einsum(
            "tj,td->jd", spread.astype(jnp.bfloat16), normed, preferred_element_type=jnp.float32
        ).astype(jnp.bfloat16)
        incoming = lax.all_to_all(
            outgoing.reshape(expert_count, CAP, model_width),
            "expert",
            split_axis=0,
            concat_axis=0,
            tiled=True,
        ).reshape(slot_count, model_width)
        expert_out, gate_pre, up_pre, hidden = lax.cond(
            is_valid,
            lambda: expert_forward(incoming, gate_map, up_map, down_map),
            lambda: spare_forward(slot_count, model_width, hidden_units),
        )
        returned = lax.all_to_all(
            expert_out.reshape(expert_count, CAP, model_width),
            "expert",
            split_axis=0,
            concat_axis=0,
            tiled=True,
        ).reshape(slot_count, model_width)
        mixed = jnp.dot(combine, returned.astype(jnp.float32), precision=BEST)
        layer_output = (wide_input + mixed).astype(jnp.bfloat16)
        stash_input = store_micro(stash_input, position, layer_input, is_valid)
        stash_rows = store_micro(stash_rows, position, incoming, is_valid)
        stash_gate = store_micro(stash_gate, position, gate_pre, is_valid)
        stash_up = store_micro(stash_up, position, up_pre, is_valid)
        stash_hidden = store_micro(stash_hidden, position, hidden, is_valid)
        stash_back = store_micro(stash_back, position, returned, is_valid)
        activations = store_micro(activations, position, layer_output, is_valid)
        passed = layer_output
    stash_grad_rows = jnp.zeros((micro_count, slot_count, model_width), jnp.bfloat16)
    stash_dgate = jnp.zeros((micro_count, slot_count, hidden_units), jnp.bfloat16)
    stash_dup = jnp.zeros((micro_count, slot_count, hidden_units), jnp.bfloat16)
    router_acc = jnp.zeros((model_width, expert_count), jnp.float32)
    gain_acc = jnp.zeros((model_width,), jnp.float32)
    input_grads = jnp.zeros((micro_count, token_count, model_width), jnp.bfloat16)
    passed_grad = jnp.zeros((token_count, model_width), jnp.bfloat16)
    for moment in range(tick_count):
        if moment > 0:
            arrived = from_behind(passed_grad, "pipe", -1)
        else:
            arrived = passed_grad
        micro_index = moment - (section_count - 1 - my_section)
        is_valid = (micro_index >= 0) & (micro_index < micro_count)
        position = jnp.clip(micro_index, 0, micro_count - 1)
        upstream = jnp.where(
            my_section == section_count - 1, pick_micro(out_grad, position), arrived
        )
        layer_input = pick_micro(stash_input, position)
        micro_ids = pick_micro(routing[0], position)
        normed, wide_input, inv_rms = normalize(layer_input, gain_row)
        weights, chosen, prob_total, pick_table, onehot, spread, combine = token_plan(
            normed, router_map, micro_ids
        )
        grad_wide = upstream.astype(jnp.float32)
        sent_grad = jnp.einsum("tj,td->jd", combine, grad_wide, precision=BEST).astype(jnp.bfloat16)
        rows_grad = lax.all_to_all(
            sent_grad.reshape(expert_count, CAP, model_width),
            "expert",
            split_axis=0,
            concat_axis=0,
            tiled=True,
        ).reshape(slot_count, model_width)
        returned = pick_micro(stash_back, position)
        slot_score = jnp.einsum(
            "td,jd->tj", grad_wide, returned.astype(jnp.float32), precision=BEST
        )
        dweight = jnp.sum(onehot * slot_score[:, None, :], axis=-1)
        dchosen = (dweight - jnp.sum(dweight * weights, axis=-1, keepdims=True)) / prob_total
        dselect = dchosen * chosen * (1.0 - chosen)
        dlogits = jnp.sum(pick_table * dselect[..., None], axis=-2)
        gate_pre = pick_micro(stash_gate, position)
        up_pre = pick_micro(stash_up, position)
        drows, dgate, dup = lax.cond(
            is_valid,
            lambda: expert_backward(rows_grad, gate_pre, up_pre, gate_map, up_map, down_map),
            lambda: spare_backward(slot_count, model_width, hidden_units),
        )
        back_grad = lax.all_to_all(
            drows.reshape(expert_count, CAP, model_width),
            "expert",
            split_axis=0,
            concat_axis=0,
            tiled=True,
        ).reshape(slot_count, model_width)
        stash_grad_rows = store_micro(stash_grad_rows, position, rows_grad, is_valid)
        stash_dgate = store_micro(stash_dgate, position, dgate, is_valid)
        stash_dup = store_micro(stash_dup, position, dup, is_valid)
        dnormed = jnp.einsum(
            "tj,jd->td", spread.astype(jnp.bfloat16), back_grad, preferred_element_type=jnp.float32
        ) + jnp.dot(dlogits, router_map.astype(jnp.float32).T, precision=BEST)
        router_term = jnp.dot(normed.astype(jnp.float32).T, dlogits, precision=BEST)
        router_acc = router_acc + jnp.where(is_valid, router_term, 0.0)
        scaled = dnormed * gain_row
        dinput = inv_rms * (
            scaled
            - wide_input
            * (inv_rms * inv_rms)
            * jnp.mean(scaled * wide_input, axis=-1, keepdims=True)
        )
        gain_term = jnp.sum(dnormed * wide_input * inv_rms, axis=0)
        gain_acc = gain_acc + jnp.where(is_valid, gain_term, 0.0)
        layer_grad = (grad_wide + dinput).astype(jnp.bfloat16)
        input_grads = store_micro(input_grads, position, layer_grad, is_valid)
        passed_grad = layer_grad
    all_rows = micro_count * slot_count
    rows_flat = stash_rows.reshape(all_rows, model_width)
    grads_flat = stash_grad_rows.reshape(all_rows, model_width)
    hidden_flat = stash_hidden.reshape(all_rows, hidden_units)
    dgate_flat = stash_dgate.reshape(all_rows, hidden_units)
    dup_flat = stash_dup.reshape(all_rows, hidden_units)
    accumulated = weight_terms(rows_flat, grads_flat, hidden_flat, dgate_flat, dup_flat)
    accumulated = (
        lax.psum_scatter(
            accumulated[0].astype(jnp.bfloat16), "dp", scatter_dimension=0, tiled=True
        ).astype(jnp.float32),
        lax.psum_scatter(
            accumulated[1].astype(jnp.bfloat16), "dp", scatter_dimension=0, tiled=True
        ).astype(jnp.float32),
        lax.psum_scatter(
            accumulated[2].astype(jnp.bfloat16), "dp", scatter_dimension=0, tiled=True
        ).astype(jnp.float32),
    )
    gate_part, up_part, down_part = accumulated
    router_part, gain_part = (
        lax.psum_scatter(router_acc, ("dp", "expert"), scatter_dimension=0, tiled=True),
        lax.psum_scatter(gain_acc, ("dp", "expert"), scatter_dimension=0, tiled=True),
    )
    return (
        activations[None],
        input_grads[None],
        gate_part.astype(jnp.bfloat16)[None, None],
        up_part.astype(jnp.bfloat16)[None, None],
        down_part.T.astype(jnp.bfloat16)[None, None],
        router_part[None],
        gain_part[None],
    )


def solution(mesh):
    return jax.shard_map(
        local,
        mesh=mesh,
        in_specs=(
            P(None, ("dp", "expert"), None),
            P(None, ("dp", "expert"), None),
            P("pipe", None),
            P("pipe", None, None),
            P("pipe", "expert", None, None),
            P("pipe", "expert", None, None),
            P("pipe", "expert", None, None),
            P("pipe", None, ("dp", "expert"), None),
        ),
        out_specs=(
            P("pipe", None, ("dp", "expert"), None),
            P("pipe", None, ("dp", "expert"), None),
            P("pipe", "expert", "dp", None),
            P("pipe", "expert", "dp", None),
            P("pipe", "expert", None, "dp"),
            P("pipe", ("dp", "expert"), None),
            P("pipe", ("dp", "expert")),
        ),
        check_vma=False,
    )
```

profile of v0, /device:TPU:1, one launch (start us, length us, event | category | flops | bytes accessed | tf_op | source)
XLA Modules:
  0.0 990.3 jit_solution(11872169961071312099)
XLA Ops:
  13.5 10.0 %all-to-all-start = ((bf16[16,8,2048]{2,1,0:T(8,128)(2,1)}), bf16[16,8,2048]{2,1,0:T(8,128)(2,1)}, u32[]{:S(2)}, u32[]{:S(2)}) async-start(bf16[16,8,2048]{2,1,0:T(8,128)(2,1)} %fusion.102), calls=%async_computation | async-start | bytes 1048576 | tf_op jit(solution)/shard_map/all_to_all | solution.py:152
  23.5 17.4 %all-to-all-done = bf16[16,8,2048]{2,1,0:T(8,128)(2,1)} async-done(((bf16[16,8,2048]{2,1,0:T(8,128)(2,1)}), bf16[16,8,2048]{2,1,0:T(8,128)(2,1)}, u32[]{:S(2)}, u32[]{:S(2)}) %all-to-all-start) | async-done | bytes 524320 | tf_op jit(solution)/shard_map/all_to_all | solution.py:152
  41.0 7.7 conditional.12
  55.0 14.8 %all-to-all-done.1 = bf16[16,8,2048]{2,1,0:T(8,128)(2,1)} async-done(((bf16[16,8,2048]{2,1,0:T(8,128)(2,1)}), bf16[16,8,2048]{2,1,0:T(8,128)(2,1)}, u32[]{:S(2)}, u32[]{:S(2)}) %all-to-all-start.1) | async-done | bytes 524320 | tf_op jit(solution)/shard_map/all_to_all | solution.py:164
  83.8 15.4 %all-to-all-done.2 = bf16[16,8,2048]{2,1,0:T(8,128)(2,1)} async-done(((bf16[16,8,2048]{2,1,0:T(8,128)(2,1)}), bf16[16,8,2048]{2,1,0:T(8,128)(2,1)}, u32[]{:S(2)}, u32[]{:S(2)}) %all-to-all-start.2) | async-done | bytes 524320 | tf_op jit(solution)/shard_map/all_to_all | solution.py:152
  99.2 6.8 conditional.13
  129.1 4.7 collective-permute-start.1
  150.5 4.6 all-to-all-start.4
  167.5 5.1 all-to-all-done.4
  172.6 6.8 conditional.14
  180.2 4.1 all-to-all-start.5
  191.0 9.5 all-to-all-done.5
  218.9 4.3 all-to-all-start.6
  232.5 7.1 all-to-all-done.6
  242.7 4.1 all-to-all-start.7
  255.6 7.5 all-to-all-done.7
  264.4 6.9 collective-permute-start.3
  290.1 7.6 all-to-all-done.8
  313.9 7.3 all-to-all-done.9
  329.3 4.1 all-to-all-start.10
  341.0 8.9 all-to-all-done.10
  353.0 4.1 all-to-all-start.11
  360.8 12.5 %all-to-all-done.11 = bf16[16,8,2048]{2,1,0:T(8,128)(2,1)} async-done(((bf16[16,8,2048]{2,1,0:T(8,128)(2,1)}), bf16[16,8,2048]{2,1,0:T(8,128)(2,1)}, u32[]{:S(2)}, u32[]{:S(2)}) %all-to-all-start.11) | async-done | bytes 524320 | tf_op jit(solution)/shard_map/all_to_all | solution.py:164
  388.0 10.7 %all-to-all-done.12 = bf16[16,8,2048]{2,1,0:T(8,128)(2,1)} async-done(((bf16[16,8,2048]{2,1,0:T(8,128)(2,1)}), bf16[16,8,2048]{2,1,0:T(8,128)(2,1)}, u32[]{:S(2)}, u32[]{:S(2)}) %all-to-all-start.12) | async-done | bytes 524320 | tf_op jit(solution)/shard_map/all_to_all | solution.py:207
  401.1 4.3 all-to-all-start.13
  410.9 10.7 %all-to-all-done.13 = bf16[16,8,2048]{2,1,0:T(8,128)(2,1)} async-done(((bf16[16,8,2048]{2,1,0:T(8,128)(2,1)}), bf16[16,8,2048]{2,1,0:T(8,128)(2,1)}, u32[]{:S(2)}, u32[]{:S(2)}) %all-to-all-start.13) | async-done | bytes 524320 | tf_op jit(solution)/shard_map/all_to_all | solution.py:229
  427.4 5.4 collective-permute-done.5
  447.9 11.0 %all-to-all-done.14 = bf16[16,8,2048]{2,1,0:T(8,128)(2,1)} async-done(((bf16[16,8,2048]{2,1,0:T(8,128)(2,1)}), bf16[16,8,2048]{2,1,0:T(8,128)(2,1)}, u32[]{:S(2)}, u32[]{:S(2)}) %all-to-all-start.14) | async-done | bytes 524320 | tf_op jit(solution)/shard_map/all_to_all | solution.py:207
  461.2 4.1 all-to-all-start.15
  471.2 10.3 %all-to-all-done.15 = bf16[16,8,2048]{2,1,0:T(8,128)(2,1)} async-done(((bf16[16,8,2048]{2,1,0:T(8,128)(2,1)}), bf16[16,8,2048]{2,1,0:T(8,128)(2,1)}, u32[]{:S(2)}, u32[]{:S(2)}) %all-to-all-start.15) | async-done | bytes 524320 | tf_op jit(solution)/shard_map/all_to_all | solution.py:229
  494.2 4.1 all-to-all-start.16
  503.8 11.5 %all-to-all-done.16 = bf16[16,8,2048]{2,1,0:T(8,128)(2,1)} async-done(((bf16[16,8,2048]{2,1,0:T(8,128)(2,1)}), bf16[16,8,2048]{2,1,0:T(8,128)(2,1)}, u32[]{:S(2)}, u32[]{:S(2)}) %all-to-all-start.16) | async-done | bytes 524320 | tf_op jit(solution)/shard_map/all_to_all | solution.py:207
  527.7 10.3 %all-to-all-done.17 = bf16[16,8,2048]{2,1,0:T(8,128)(2,1)} async-done(((bf16[16,8,2048]{2,1,0:T(8,128)(2,1)}), bf16[16,8,2048]{2,1,0:T(8,128)(2,1)}, u32[]{:S(2)}, u32[]{:S(2)}) %all-to-all-start.17) | async-done | bytes 524320 | tf_op jit(solution)/shard_map/all_to_all | solution.py:229
  543.9 25.3 %collective-permute-done.7 = bf16[8,2048]{1,0:T(8,128)(2,1)S(1)} collective-permute-done((bf16[8,2048]{1,0:T(8,128)(2,1)S(1)}, bf16[8,2048]{1,0:T(8,128)(2,1)S(1)}, u32[]{:S(2)}, u32[]{:S(2)}) %collective-permute-start.7) | collective-permute-done | bytes 32800 | tf_op jit(solution)/shard_map/ppermute | solution.py:16
  582.4 12.3 %all-to-all-done.18 = bf16[16,8,2048]{2,1,0:T(8,128)(2,1)} async-done(((bf16[16,8,2048]{2,1,0:T(8,128)(2,1)}), bf16[16,8,2048]{2,1,0:T(8,128)(2,1)}, u32[]{:S(2)}, u32[]{:S(2)}) %all-to-all-start.18) | async-done | bytes 524320 | tf_op jit(solution)/shard_map/all_to_all | solution.py:207
  594.7 8.5 conditional.21
  594.7 4.2 fusion.70
  614.0 10.3 %all-to-all-done.19 = bf16[16,8,2048]{2,1,0:T(8,128)(2,1)} async-done(((bf16[16,8,2048]{2,1,0:T(8,128)(2,1)}), bf16[16,8,2048]{2,1,0:T(8,128)(2,1)}, u32[]{:S(2)}, u32[]{:S(2)}) %all-to-all-start.19) | async-done | bytes 524320 | tf_op jit(solution)/shard_map/all_to_all | solution.py:229
  646.3 11.8 %all-to-all-done.20 = bf16[16,8,2048]{2,1,0:T(8,128)(2,1)} async-done(((bf16[16,8,2048]{2,1,0:T(8,128)(2,1)}), bf16[16,8,2048]{2,1,0:T(8,128)(2,1)}, u32[]{:S(2)}, u32[]{:S(2)}) %all-to-all-start.20) | async-done | bytes 524320 | tf_op jit(solution)/shard_map/all_to_all | solution.py:207
  658.1 8.5 conditional.22
  658.1 4.2 fusion.82
  676.5 11.3 %all-to-all-done.21 = bf16[16,8,2048]{2,1,0:T(8,128)(2,1)} async-done(((bf16[16,8,2048]{2,1,0:T(8,128)(2,1)}), bf16[16,8,2048]{2,1,0:T(8,128)(2,1)}, u32[]{:S(2)}, u32[]{:S(2)}) %all-to-all-start.21) | async-done | bytes 524320 | tf_op jit(solution)/shard_map/all_to_all | solution.py:229
  711.1 11.1 %all-to-all-done.22 = bf16[16,8,2048]{2,1,0:T(8,128)(2,1)} async-done(((bf16[16,8,2048]{2,1,0:T(8,128)(2,1)}), bf16[16,8,2048]{2,1,0:T(8,128)(2,1)}, u32[]{:S(2)}, u32[]{:S(2)}) %all-to-all-start.22) | async-done | bytes 524320 | tf_op jit(solution)/shard_map/all_to_all | solution.py:207
  724.4 5.1 bitcast_convert_fusion
  741.7 8.2 conditional.23
  751.7 5.1 bitcast_convert_fusion.2
  770.3 74.7 %reduce-scatter.13.cloned.1.call-done = f32[32,16]{1,0:T(8,128)} async-done(((f32[2048,16]{1,0:T(8,128)}), f32[32,16]{1,0:T(8,128)}) %reduce-scatter.13.cloned.1.call-update) | async-done | bytes 2064
  847.0 133.6 %all-reduce = f32[2048]{0:T(1024)S(1)} all-reduce(f32[2048]{0:T(1024)S(1)} %select_add_fusion), channel_id=6, replica_groups=mesh['dp'=4,'pipe'=4,'expert'=16] {'dp','expert'}, use_global_device_ids=true, to_apply=%region_142.143.clone | all-reduce | flops 2048 | bytes 16384
  (576 shorter events, 433.6 us)
Async XLA Ops:
  9.7 64.0 %copy-start.56 = (s32[1,1,8,8]{3,2,1,0:T(8,128)}, s32[1,1,8,8]{3,2,1,0:T(8,128)S(1)}, u32[]{:S(2)}) copy-start(s32[1,1,8,8]{3,2,1,0:T(8,128)S(1)} %get-tuple-element.687) | copy-start | bytes 772
  13.5 27.4 %all-to-all-start = ((bf16[16,8,2048]{2,1,0:T(8,128)(2,1)}), bf16[16,8,2048]{2,1,0:T(8,128)(2,1)}, u32[]{:S(2)}, u32[]{:S(2)}) async-start(bf16[16,8,2048]{2,1,0:T(8,128)(2,1)} %fusion.102), calls=%async_computation | async-start | bytes 1048576 | tf_op jit(solution)/shard_map/all_to_all | solution.py:152
  49.5 20.3 %all-to-all-start.1 = ((bf16[16,8,2048]{2,1,0:T(8,128)(2,1)}), bf16[16,8,2048]{2,1,0:T(8,128)(2,1)}, u32[]{:S(2)}, u32[]{:S(2)}) async-start(bf16[16,8,2048]{2,1,0:T(8,128)(2,1)} %bitcast.1360), calls=%async_computation.1 | async-start | bytes 1048576 | tf_op jit(solution)/shard_map/all_to_all | solution.py:164
  71.8 2.6 collective-permute-start
  78.3 20.9 %all-to-all-start.2 = ((bf16[16,8,2048]{2,1,0:T(8,128)(2,1)}), bf16[16,8,2048]{2,1,0:T(8,128)(2,1)}, u32[]{:S(2)}, u32[]{:S(2)}) async-start(bf16[16,8,2048]{2,1,0:T(8,128)(2,1)} %fusion.103), calls=%async_computation.2 | async-start | bytes 1048576 | tf_op jit(solution)/shard_map/all_to_all | solution.py:152
  106.8 20.4 %all-to-all-start.3 = ((bf16[16,8,2048]{2,1,0:T(8,128)(2,1)}), bf16[16,8,2048]{2,1,0:T(8,128)(2,1)}, u32[]{:S(2)}, u32[]{:S(2)}) async-start(bf16[16,8,2048]{2,1,0:T(8,128)(2,1)} %bitcast.1361), calls=%async_computation.3 | async-start | bytes 1048576 | tf_op jit(solution)/shard_map/all_to_all | solution.py:164
  129.1 16.9 %collective-permute-start.1 = (bf16[8,2048]{1,0:T(8,128)(2,1)}, bf16[8,2048]{1,0:T(8,128)(2,1)S(1)}, u32[]{:S(2)}, u32[]{:S(2)}) collective-permute-start(bf16[8,2048]{1,0:T(8,128)(2,1)} %get-tuple-element.705), channel_id=1, source_target_pairs={{0,16},{16,32},{32,48},{1,17},{17,33},{33,49},{2,18},{18,34},{34,5... | collective-permute-start | bytes 98312 | tf_op jit(solution)/shard_map/ppermute | solution.py:16
  150.5 22.1 %all-to-all-start.4 = ((bf16[16,8,2048]{2,1,0:T(8,128)(2,1)}), bf16[16,8,2048]{2,1,0:T(8,128)(2,1)}, u32[]{:S(2)}, u32[]{:S(2)}) async-start(bf16[16,8,2048]{2,1,0:T(8,128)(2,1)} %fusion.104), calls=%async_computation.4 | async-start | bytes 1048576 | tf_op jit(solution)/shard_map/all_to_all | solution.py:152
  180.2 20.3 %all-to-all-start.5 = ((bf16[16,8,2048]{2,1,0:T(8,128)(2,1)}), bf16[16,8,2048]{2,1,0:T(8,128)(2,1)}, u32[]{:S(2)}, u32[]{:S(2)}) async-start(bf16[16,8,2048]{2,1,0:T(8,128)(2,1)} %bitcast.1362), calls=%async_computation.5 | async-start | bytes 1048576 | tf_op jit(solution)/shard_map/all_to_all | solution.py:164
  202.5 11.9 %collective-permute-start.2 = (bf16[8,2048]{1,0:T(8,128)(2,1)}, bf16[8,2048]{1,0:T(8,128)(2,1)S(1)}, u32[]{:S(2)}, u32[]{:S(2)}) collective-permute-start(bf16[8,2048]{1,0:T(8,128)(2,1)} %get-tuple-element.707), channel_id=1, source_target_pairs={{0,16},{16,32},{32,48},{1,17},{17,33},{33,49},{2,18},{18,34},{34,5... | collective-permute-start | bytes 98312 | tf_op jit(solution)/shard_map/ppermute | solution.py:16
  218.9 20.7 %all-to-all-start.6 = ((bf16[16,8,2048]{2,1,0:T(8,128)(2,1)}), bf16[16,8,2048]{2,1,0:T(8,128)(2,1)}, u32[]{:S(2)}, u32[]{:S(2)}) async-start(bf16[16,8,2048]{2,1,0:T(8,128)(2,1)} %fusion.105), calls=%async_computation.6 | async-start | bytes 1048576 | tf_op jit(solution)/shard_map/all_to_all | solution.py:152
  242.7 20.3 %all-to-all-start.7 = ((bf16[16,8,2048]{2,1,0:T(8,128)(2,1)}), bf16[16,8,2048]{2,1,0:T(8,128)(2,1)}, u32[]{:S(2)}, u32[]{:S(2)}) async-start(bf16[16,8,2048]{2,1,0:T(8,128)(2,1)} %bitcast.1363), calls=%async_computation.7 | async-start | bytes 1048576 | tf_op jit(solution)/shard_map/all_to_all | solution.py:164
  264.4 10.2 %collective-permute-start.3 = (bf16[8,2048]{1,0:T(8,128)(2,1)S(1)}, bf16[8,2048]{1,0:T(8,128)(2,1)S(1)}, u32[]{:S(2)}, u32[]{:S(2)}) collective-permute-start(bf16[8,2048]{1,0:T(8,128)(2,1)S(1)} %get-tuple-element.709), channel_id=1, source_target_pairs={{0,16},{16,32},{32,48},{1,17},{17,33},{33,49},{2,18},{18,34},{34,5... | collective-permute-start | bytes 98312 | tf_op jit(solution)/shard_map/ppermute | solution.py:16
  277.1 20.7 %all-to-all-start.8 = ((bf16[16,8,2048]{2,1,0:T(8,128)(2,1)}), bf16[16,8,2048]{2,1,0:T(8,128)(2,1)}, u32[]{:S(2)}, u32[]{:S(2)}) async-start(bf16[16,8,2048]{2,1,0:T(8,128)(2,1)} %fusion.106), calls=%async_computation.8 | async-start | bytes 1048576 | tf_op jit(solution)/shard_map/all_to_all | solution.py:152
  300.9 20.3 %all-to-all-start.9 = ((bf16[16,8,2048]{2,1,0:T(8,128)(2,1)}), bf16[16,8,2048]{2,1,0:T(8,128)(2,1)}, u32[]{:S(2)}, u32[]{:S(2)}) async-start(bf16[16,8,2048]{2,1,0:T(8,128)(2,1)} %bitcast.1364), calls=%async_computation.9 | async-start | bytes 1048576 | tf_op jit(solution)/shard_map/all_to_all | solution.py:164
  322.6 4.2 collective-permute-start.4
  329.3 20.6 %all-to-all-start.10 = ((bf16[16,8,2048]{2,1,0:T(8,128)(2,1)}), bf16[16,8,2048]{2,1,0:T(8,128)(2,1)}, u32[]{:S(2)}, u32[]{:S(2)}) async-start(bf16[16,8,2048]{2,1,0:T(8,128)(2,1)} %fusion.107), calls=%async_computation.10 | async-start | bytes 1048576 | tf_op jit(solution)/shard_map/all_to_all | solution.py:152
  353.0 20.3 %all-to-all-start.11 = ((bf16[16,8,2048]{2,1,0:T(8,128)(2,1)}), bf16[16,8,2048]{2,1,0:T(8,128)(2,1)}, u32[]{:S(2)}, u32[]{:S(2)}) async-start(bf16[16,8,2048]{2,1,0:T(8,128)(2,1)} %bitcast.1365), calls=%async_computation.11 | async-start | bytes 1048576 | tf_op jit(solution)/shard_map/all_to_all | solution.py:164
  378.3 20.4 %all-to-all-start.12 = ((bf16[16,8,2048]{2,1,0:T(8,128)(2,1)}), bf16[16,8,2048]{2,1,0:T(8,128)(2,1)}, u32[]{:S(2)}, u32[]{:S(2)}) async-start(bf16[16,8,2048]{2,1,0:T(8,128)(2,1)} %fusion.96), calls=%async_computation.12 | async-start | bytes 1048576 | tf_op jit(solution)/shard_map/all_to_all | solution.py:207
  401.1 20.4 %all-to-all-start.13 = ((bf16[16,8,2048]{2,1,0:T(8,128)(2,1)}), bf16[16,8,2048]{2,1,0:T(8,128)(2,1)}, u32[]{:S(2)}, u32[]{:S(2)}) async-start(bf16[16,8,2048]{2,1,0:T(8,128)(2,1)} %bitcast.1366), calls=%async_computation.13 | async-start | bytes 1048576 | tf_op jit(solution)/shard_map/all_to_all | solution.py:229
  425.3 7.6 collective-permute-start.5
  437.7 21.2 %all-to-all-start.14 = ((bf16[16,8,2048]{2,1,0:T(8,128)(2,1)}), bf16[16,8,2048]{2,1,0:T(8,128)(2,1)}, u32[]{:S(2)}, u32[]{:S(2)}) async-start(bf16[16,8,2048]{2,1,0:T(8,128)(2,1)} %fusion.97), calls=%async_computation.14 | async-start | bytes 1048576 | tf_op jit(solution)/shard_map/all_to_all | solution.py:207
  461.2 20.4 %all-to-all-start.15 = ((bf16[16,8,2048]{2,1,0:T(8,128)(2,1)}), bf16[16,8,2048]{2,1,0:T(8,128)(2,1)}, u32[]{:S(2)}, u32[]{:S(2)}) async-start(bf16[16,8,2048]{2,1,0:T(8,128)(2,1)} %bitcast.1367), calls=%async_computation.15 | async-start | bytes 1048576 | tf_op jit(solution)/shard_map/all_to_all | solution.py:229
  485.0 4.9 collective-permute-start.6
  494.2 21.2 %all-to-all-start.16 = ((bf16[16,8,2048]{2,1,0:T(8,128)(2,1)}), bf16[16,8,2048]{2,1,0:T(8,128)(2,1)}, u32[]{:S(2)}, u32[]{:S(2)}) async-start(bf16[16,8,2048]{2,1,0:T(8,128)(2,1)} %fusion.98), calls=%async_computation.16 | async-start | bytes 1048576 | tf_op jit(solution)/shard_map/all_to_all | solution.py:207
  517.6 20.4 %all-to-all-start.17 = ((bf16[16,8,2048]{2,1,0:T(8,128)(2,1)}), bf16[16,8,2048]{2,1,0:T(8,128)(2,1)}, u32[]{:S(2)}, u32[]{:S(2)}) async-start(bf16[16,8,2048]{2,1,0:T(8,128)(2,1)} %bitcast.1368), calls=%async_computation.17 | async-start | bytes 1048576 | tf_op jit(solution)/shard_map/all_to_all | solution.py:229
  541.5 27.8 %collective-permute-start.7 = (bf16[8,2048]{1,0:T(8,128)(2,1)S(1)}, bf16[8,2048]{1,0:T(8,128)(2,1)S(1)}, u32[]{:S(2)}, u32[]{:S(2)}) collective-permute-start(bf16[8,2048]{1,0:T(8,128)(2,1)S(1)} %get-tuple-element.639), channel_id=1, source_target_pairs={{16,0},{32,16},{48,32},{17,1},{33,17},{49,33},{18,2},{34,18},{50,3... | collective-permute-start | bytes 98312 | tf_op jit(solution)/shard_map/ppermute | solution.py:16
  573.5 21.2 %all-to-all-start.18 = ((bf16[16,8,2048]{2,1,0:T(8,128)(2,1)}), bf16[16,8,2048]{2,1,0:T(8,128)(2,1)}, u32[]{:S(2)}, u32[]{:S(2)}) async-start(bf16[16,8,2048]{2,1,0:T(8,128)(2,1)} %fusion.99), calls=%async_computation.18 | async-start | bytes 1048576 | tf_op jit(solution)/shard_map/all_to_all | solution.py:207
  604.0 20.4 %all-to-all-start.19 = ((bf16[16,8,2048]{2,1,0:T(8,128)(2,1)}), bf16[16,8,2048]{2,1,0:T(8,128)(2,1)}, u32[]{:S(2)}, u32[]{:S(2)}) async-start(bf16[16,8,2048]{2,1,0:T(8,128)(2,1)} %bitcast.1369), calls=%async_computation.19 | async-start | bytes 1048576 | tf_op jit(solution)/shard_map/all_to_all | solution.py:229
  627.8 4.9 collective-permute-start.8
  636.9 21.2 %all-to-all-start.20 = ((bf16[16,8,2048]{2,1,0:T(8,128)(2,1)}), bf16[16,8,2048]{2,1,0:T(8,128)(2,1)}, u32[]{:S(2)}, u32[]{:S(2)}) async-start(bf16[16,8,2048]{2,1,0:T(8,128)(2,1)} %fusion.100), calls=%async_computation.20 | async-start | bytes 1048576 | tf_op jit(solution)/shard_map/all_to_all | solution.py:207
  667.4 20.4 %all-to-all-start.21 = ((bf16[16,8,2048]{2,1,0:T(8,128)(2,1)}), bf16[16,8,2048]{2,1,0:T(8,128)(2,1)}, u32[]{:S(2)}, u32[]{:S(2)}) async-start(bf16[16,8,2048]{2,1,0:T(8,128)(2,1)} %bitcast.1370), calls=%async_computation.21 | async-start | bytes 1048576 | tf_op jit(solution)/shard_map/all_to_all | solution.py:229
  691.3 4.9 collective-permute-start.9
  701.1 21.2 %all-to-all-start.22 = ((bf16[16,8,2048]{2,1,0:T(8,128)(2,1)}), bf16[16,8,2048]{2,1,0:T(8,128)(2,1)}, u32[]{:S(2)}, u32[]{:S(2)}) async-start(bf16[16,8,2048]{2,1,0:T(8,128)(2,1)} %fusion.101), calls=%async_computation.22 | async-start | bytes 1048576 | tf_op jit(solution)/shard_map/all_to_all | solution.py:207
  705.2 139.8 %reduce-scatter.13.cloned.1.call-start = ((), (), s32[]{:S(2)}) async-start(), calls=%async_computation.31 | async-start | bytes 1064960
  711.1 270.2 %reduce-scatter.11.cloned.1.call-start = ((), (), s32[]{:S(2)}) async-start(), calls=%async_computation.30 | async-start | bytes 3932160 | tf_op jit(solution)/shard_map/reduce_scatter | solution.py:270
  729.5 254.1 %reduce-scatter.7.cloned.1.call-start = ((), (), s32[]{:S(2)}) async-start(), calls=%async_computation.28 | async-start | bytes 3932160 | tf_op jit(solution)/shard_map/reduce_scatter | solution.py:264
  756.8 226.8 %reduce-scatter.9.cloned.1.call-start = ((), (), s32[]{:S(2)}) async-start(), calls=%async_computation.29 | async-start | bytes 3932160 | tf_op jit(solution)/shard_map/reduce_scatter | solution.py:267
  763.9 82.5 %copy-start.80 = (bf16[8,128]{1,0:T(8,128)(2,1)S(1)}, bf16[8,128]{1,0:T(8,128)(2,1)}, u32[]{:S(2)}) copy-start(bf16[8,128]{1,0:T(8,128)(2,1)} %get-tuple-element.606) | copy-start | bytes 6148
  763.9 82.7 %copy-start.89 = (f32[8]{0:T(128)S(1)}, f32[8]{0:T(128)}, u32[]{:S(2)}) copy-start(f32[8]{0:T(128)} %copy-done.87) | copy-start | bytes 100
  763.9 83.0 %copy-start.67 = (f32[2048]{0:T(1024)S(1)}, f32[2048]{0:T(1024)}, u32[]{:S(2)}) copy-start(f32[2048]{0:T(1024)} %get-tuple-element.563) | copy-start | bytes 24580
  763.9 83.0 %copy-start.68 = (f32[2048]{0:T(1024)S(1)}, f32[2048]{0:T(1024)}, u32[]{:S(2)}) copy-start(f32[2048]{0:T(1024)} %get-tuple-element.565) | copy-start | bytes 24580
  763.9 83.0 %copy-start.69 = (f32[2048]{0:T(1024)S(1)}, f32[2048]{0:T(1024)}, u32[]{:S(2)}) copy-start(f32[2048]{0:T(1024)} %get-tuple-element.567) | copy-start | bytes 24580
  764.0 83.0 %copy-start.70 = (f32[2048]{0:T(1024)S(1)}, f32[2048]{0:T(1024)}, u32[]{:S(2)}) copy-start(f32[2048]{0:T(1024)} %get-tuple-element.569) | copy-start | bytes 24580
  764.0 83.0 %copy-start.71 = (f32[2048]{0:T(1024)S(1)}, f32[2048]{0:T(1024)}, u32[]{:S(2)}) copy-start(f32[2048]{0:T(1024)} %get-tuple-element.571) | copy-start | bytes 24580
  764.0 217.2 %copy-start.97 = (f32[8]{0:T(128)S(1)}, f32[8]{0:T(128)}, u32[]{:S(2)}) copy-start(f32[8]{0:T(128)} %get-tuple-element.690) | copy-start | bytes 100
  764.0 82.4 %all-to-all-start.23 = ((bf16[16,8,2048]{2,1,0:T(8,128)(2,1)}), bf16[16,8,2048]{2,1,0:T(8,128)(2,1)S(1)}, u32[]{:S(2)}, u32[]{:S(2)}) async-start(bf16[16,8,2048]{2,1,0:T(8,128)(2,1)} %bitcast.165), calls=%async_computation.23 | async-start | bytes 1048576 | tf_op jit(solution)/shard_map/all_to_all | solution.py:229
  770.3 213.3 %copy-start.52 = (bf16[1,3,8,2048]{3,2,1,0:T(8,128)(2,1)}, bf16[1,3,8,2048]{3,2,1,0:T(8,128)(2,1)S(1)}, u32[]{:S(2)}) copy-start(bf16[1,3,8,2048]{3,2,1,0:T(8,128)(2,1)S(1)} %fusion.121) | copy-start | bytes 294916
  (80 other events, 492.1 us)
Sparse Core Ops, SparseCore 0:
  711.2 133.7 reduce-scatter.12
  847.5 45.0 reduce-scatter.10
  895.8 40.5 reduce-scatter.6
  939.4 40.6 reduce-scatter.8
where the time goes:
time: 1010 us; the launch traced here: 990 us
  waiting for transfers between devices  348 us (34%)
  other arithmetic  160 us (16%)
  blocking collectives  134 us (13%)
  starting transfers between devices  131 us (13%)
  matrix products  120 us (12%)
  local copies, waits for them, and re-layouts  80.8 us (8%)
  between operations  16.1 us (2%)
    unnamed x1, blocking collectives  134 us
    unnamed x5, waiting for transfers between devices  74.8 us
    all_to_all x6, waiting for transfers between devices, local(): lax.all_to_all(sent_grad.reshape(expert_count, CAP, model_width), 'expert...  68.4 us
    dynamic_update_slice x60, other arithmetic, store_micro(): lax.dynamic_update_index_in_dim(stored, jnp.where(is_valid, fresh, previo...  67.5 us
    all_to_all x6, waiting for transfers between devices, local(): lax.all_to_all(outgoing.reshape(expert_count, CAP, model_width), 'expert'...  61.6 us
    all_to_all x6, waiting for transfers between devices, local(): lax.all_to_all(expert_out.reshape(expert_count, CAP, model_width), 'exper...  53.2 us
    all_to_all x6, waiting for transfers between devices, local(): lax.all_to_all(drows.reshape(expert_count, CAP, model_width), 'expert', s...  52.9 us
    ppermute x10, waiting for transfers between devices, from_behind(): lax.ppermute(value, axis, [(source, source + steps) for source in range(f...  37.4 us
  transfers between devices with their start and end apart: 38, of which 30 were waited for; matrix products, arithmetic and copies ran while one was open for 22% of the time, Pallas kernels for 0%

commit v1 on v0

v1 whole, which is shorter than its diff:
```python
import functools

import jax
import jax.numpy as jnp
from jax import lax
from jax.experimental import pallas as pl
from jax.experimental.pallas import tpu as pltpu
from jax.sharding import PartitionSpec as P

EPSILON = 1e-06
MESH = pl.DeviceIdType.MESH
BF = jnp.bfloat16
F32 = jnp.float32
NN = (((1,), (0,)), ((), ()))
NT = (((1,), (1,)), ((), ()))
TN = (((0,), (0,)), ((), ()))


def dot(a, b, dims):
    return lax.dot_general(a, b, dims, preferred_element_type=F32)


def col(value):
    return jnp.sum(value, axis=-1, keepdims=True)


def kernel(
    sizes,
    emb_ref, og_ref, ids_ref, gain_ref, rw_ref, gate_hbm, up_hbm, down_hbm,
    act_ref, igr_ref, gg_ref, ug_ref, dg_ref, rg_ref,
    wg, wu, wd, ebs, ebr, src0, pmall, xall, nrm, gpre, upre, hidb, invs, wst, lgs,
    ps_f, pr_f, ps_b, pr_b, qo_f, qo_b, qf, qb, rf, rb, actb,
    nsl, gsl, hid, dga, dup, racc, rgs, ybuf, ysum, zbuf,
    w_sem, e_s, e_r, m_s, m_r, ag0_s, ag_s, ag_r, fw_s, fw_r, pr_s, pr_rs, rs_s, rs_r, ac_s, ac_r,
    y_s, y_r, r1_s, r1_r, r2_s, r2_r,
):
    NM, D, F, NE, ND, NP = sizes
    NZ, H, R, DS = NE // 2, D // 2, NE * 8, D // ND
    HX = H + 128
    me_y = lax.axis_index("dp")
    me_l = lax.axis_index("pipe")
    me_e = lax.axis_index("expert")
    z = me_e // 2
    c = me_e % 2
    oc = 1 - c
    partner = {"expert": me_e + 1 - 2 * c}
    own_rows = pl.ds(pl.multiple_of(z * 16, 16), 16)
    own_half = pl.ds(pl.multiple_of(c * H, H), H)
    other_half = pl.ds(pl.multiple_of(oc * H, H), H)
    last = (me_l + 1) // NP

    def send(src, dst, ss, rs, dev):
        pltpu.make_async_remote_copy(
            src_ref=src, dst_ref=dst, send_sem=ss, recv_sem=rs, device_id=dev, device_id_type=MESH
        ).start()

    def copy(src, dst, sem):
        pltpu.make_async_copy(src, dst, sem).start()

    def wait(ref, sem):
        pltpu.make_async_copy(ref, ref, sem).wait()

    copy(gate_hbm, wg, w_sem.at[0])
    copy(up_hbm, wu, w_sem.at[1])
    copy(down_hbm, wd, w_sem.at[2])

    barrier = pltpu.get_barrier_semaphore()

    def hello(dev):
        pl.semaphore_signal(barrier, inc=1, device_id=dev, device_id_type=MESH)

    hello(partner)
    for k in range(1, NZ):
        for cc in range(2):
            hello({"expert": 2 * ((z + k) % NZ) + cc})
    for j in range(1, ND):
        hello({"dp": (me_y + j) % ND})
    for step in (1, NP - 1):
        for k in range(NZ):
            hello({"pipe": (me_l + step) % NP, "expert": 2 * ((z + k) % NZ) + c})

    mine0 = (c == 0).astype(F32)
    for kind, ref in enumerate((emb_ref, og_ref)):
        for m in range(NM):
            v = ref[m].astype(F32)
            blk = jnp.concatenate([v * mine0, v * (1.0 - mine0)], axis=0).astype(BF)
            ebs[kind, 0, m] = blk[:, :H]
            ebs[kind, 1, m] = blk[:, H:]
    lanes8 = lax.broadcasted_iota(jnp.int32, (8, 128), 1)
    for m in range(NM):
        ids = ids_ref[m]
        table = jnp.zeros((8, 128), F32)
        for k in range(ids.shape[1]):
            table = table + (ids[:, k:k + 1] == lanes8).astype(F32)
        pmall[me_e, m] = table
    racc[...] = jnp.zeros(racc.shape, F32)

    pl.semaphore_wait(barrier, 1 + 2 * (NZ - 1) + (ND - 1) + 2 * NZ)

    for kind in range(2):
        send(ebs.at[kind, oc], ebr.at[kind], e_s.at[kind], e_r.at[kind], partner)
    send(pmall.at[me_e], pmall.at[me_e], m_s, m_r, partner)
    for k in range(1, NZ):
        for cc in range(2):
            send(
                pmall.at[me_e], pmall.at[me_e], m_s, m_r, {"expert": 2 * ((z + k) % NZ) + cc}
            )

    def gather_here(kind, m):
        src = src0.at[kind, m]
        dst = xall.at[kind, m, c, own_rows]
        for k in range(1, NZ):
            send(src, dst, ag0_s.at[kind, m], ag_r.at[kind, m], {"expert": 2 * ((z + k) % NZ) + c})
        copy(src, dst, ag_r.at[kind, m])

    def gather_there(kind, m, section):
        for k in range(NZ):
            send(
                actb.at[kind, c, m], xall.at[kind, m, c, own_rows],
                ag_s.at[kind, m], ag_r.at[kind, m],
                {"pipe": section, "expert": 2 * ((z + k) % NZ) + c},
            )

    for kind in range(2):
        wait(ebr.at[kind], e_r.at[kind])
        for m in range(NM):
            src0[kind, m] = (
                ebs[kind, c, m].astype(F32) + ebr[kind, m].astype(F32)
            ).astype(BF)
        if kind == 0:
            @pl.when(me_l == 0)
            def _():
                gather_here(0, 0)
        else:
            @pl.when(last == 1)
            def _():
                for m in range(NM):
                    gather_here(1, m)

    wait(pmall.at[pl.ds(0, NE - 1)], m_r)
    wait(wg, w_sem.at[0])
    wait(wu, w_sem.at[1])
    wait(wd, w_sem.at[2])

    def arrive(kind, m):
        wait(xall.at[kind, m, c], ag_r.at[kind, m])
        send(
            xall.at[kind, m, c], xall.at[kind, m, c], fw_s.at[kind, m], fw_r.at[kind, m], partner
        )
        if kind == 0:
            @pl.when((me_l == 0) & (m < NM - 1))
            def _():
                gather_here(0, m + 1)
        wait(xall.at[kind, m, oc], fw_r.at[kind, m])

    lane_e = lax.broadcasted_iota(jnp.int32, (R, NE), 1)
    lane_x = lax.broadcasted_iota(jnp.int32, (R, 128), 1)

    def forward_compute(m):
        x0 = xall[0, m, 0].astype(F32)
        x1 = xall[0, m, 1].astype(F32)
        inv = lax.rsqrt((col(x0 * x0) + col(x1 * x1)) * (1.0 / D) + EPSILON)
        n0 = (x0 * inv * gain_ref[0:1, :H]).astype(BF)
        n1 = (x1 * inv * gain_ref[0:1, H:]).astype(BF)
        nrm[m, 0] = n0
        nrm[m, 1] = n1
        logits = dot(n0, rw_ref[:H, :], NN) + dot(n1, rw_ref[H:, :], NN)
        named = pmall[:, m].reshape(R, 128)[:, :NE]
        chosen = named * jax.nn.sigmoid(logits)
        w = col(jnp.where(lane_e == me_e, chosen, 0.0)) / col(chosen)
        invs[m] = jnp.broadcast_to(inv, (R, 128))
        wst[m] = jnp.broadcast_to(w, (R, 128))
        lgs[m] = logits
        a = dot(n0, wg[:H, :], NN) + dot(n1, wg[H:, :], NN)
        b = dot(n0, wu[:H, :], NN) + dot(n1, wu[H:, :], NN)
        gpre[m] = a
        upre[m] = b
        h = (a * jax.nn.sigmoid(a) * b).astype(BF)
        hidb[m] = h
        hid[me_y, m] = (h.astype(F32) * w).astype(BF)
        ps_f[m] = (dot(h, wd[:, other_half], NN) * w).astype(BF)
        send(ps_f.at[m], pr_f.at[m], pr_s.at[0, m], pr_rs.at[0, m], partner)
        qo_f[...] = dot(h, wd[:, own_half], NN) * w

    def scatter(kind, m, q, r):
        for k in range(1, NZ):
            zz = (z + k) % NZ
            send(
                q.at[m, pl.ds(pl.multiple_of(zz * 16, 16), 16)], r.at[m, z],
                rs_s.at[kind, m], rs_r.at[kind, m], {"expert": 2 * zz + c},
            )
        copy(q.at[m, own_rows], r.at[m, z], rs_r.at[kind, m])

    def half_slice(ref, yy):
        start = yy * DS
        return ref.at[start // H, :, pl.ds(pl.multiple_of(start % H, 128), DS)]

    def to_replicas(m, whole, halves, slices, base):
        for j in range(1, ND):
            yy = (me_y + j) % ND
            for i, ref in enumerate(whole):
                send(
                    ref.at[me_y, m], ref.at[me_y, m], y_s.at[base + i, m], y_r.at[base + i, m],
                    {"dp": yy},
                )
            i = base + len(whole)
            send(half_slice(halves, yy), slices.at[me_y, m], y_s.at[i, m], y_r.at[i, m], {"dp": yy})
        i = base + len(whole)
        copy(half_slice(halves, me_y), slices.at[me_y, m], y_r.at[i, m])

    def forward_scatter(m):
        wait(pr_f.at[m], pr_rs.at[0, m])
        qf[m] = (qo_f[...] + pr_f[m].astype(F32)).astype(BF)
        scatter(0, m, qf, rf)
        to_replicas(m, (hid,), nrm.at[m], nsl, 0)

    def forward_result(m):
        wait(rf.at[m], rs_r.at[0, m])
        total = xall[0, m, c, own_rows].astype(F32)
        for k in range(NZ):
            total = total + rf[m, k].astype(F32)
        actb[0, c, m] = total.astype(BF)

        @pl.when(last == 0)
        def _():
            gather_there(0, m, me_l + 1)

        send(actb.at[0, c, m], actb.at[0, c, m], ac_s.at[0, m], ac_r.at[0, m], partner)

    def backward_compute(m):
        dh = dot(xall[1, m, 0], wd[:, :H], NT) + dot(xall[1, m, 1], wd[:, H:], NT)
        w = wst[m][:, :1]
        a = gpre[m]
        b = upre[m]
        dw = col(dh * hidb[m].astype(F32))
        dhw = dh * w
        s = jax.nn.sigmoid(a)
        dgate = (dhw * b * s * (1.0 + a * (1.0 - s))).astype(BF)
        dupv = (dhw * (a * s)).astype(BF)
        dga[me_y, m] = dgate
        dup[me_y, m] = dupv
        sv = col(dgate.astype(F32) * a + dupv.astype(F32) * b)
        dw_hi = dw.astype(BF).astype(F32)
        sv_hi = sv.astype(BF).astype(F32)
        ext = jnp.where(lane_x == me_e, dw_hi, 0.0)
        ext = jnp.where(lane_x == NE + me_e, dw - dw_hi, ext)
        ext = jnp.where(lane_x == 2 * NE + me_e, sv_hi, ext)
        ext = jnp.where(lane_x == 3 * NE + me_e, sv - sv_hi, ext)
        ps_b[m, :, :H] = (
            dot(dgate, wg[other_half, :], NT) + dot(dupv, wu[other_half, :], NT)
        ).astype(BF)
        ps_b[m, :, H:] = ext.astype(BF)
        send(ps_b.at[m], pr_b.at[m], pr_s.at[1, m], pr_rs.at[1, m], partner)
        qo_b[:, :H] = dot(dgate, wg[own_half, :], NT) + dot(dupv, wu[own_half, :], NT)
        qo_b[:, H:] = ext

    def backward_scatter(m):
        wait(pr_b.at[m], pr_rs.at[1, m])
        qb[m] = (qo_b[...] + pr_b[m].astype(F32)).astype(BF)
        scatter(1, m, qb, rb)
        to_replicas(m, (dga, dup), xall.at[1, m], gsl, 2)

    def backward_result(m):
        wait(rb.at[m], rs_r.at[1, m])
        total = rb[m, 0].astype(F32)
        for k in range(1, NZ):
            total = total + rb[m, k].astype(F32)
        ext = total[:, H:]
        dw = ext[:, :NE] + ext[:, NE:2 * NE]
        sv = col(ext[:, 2 * NE:3 * NE] + ext[:, 3 * NE:4 * NE])
        logits = lgs[m, own_rows]
        named = pmall[pl.ds(2 * z, 2), m].reshape(16, 128)[:, :NE]
        chosen = named * jax.nn.sigmoid(logits)
        prob_total = col(chosen)
        weights = chosen / prob_total
        dchosen = (dw - col(dw * weights)) / prob_total
        dlogits = dchosen * chosen * (1.0 - chosen)
        dl_hi = dlogits.astype(BF)
        dl_lo = (dlogits - dl_hi.astype(F32)).astype(BF)
        router_half = rw_ref[own_half, :]
        dnormed = total[:, :H] + dot(dl_hi, router_half, NT) + dot(dl_lo, router_half, NT)
        inv = invs[m, own_rows][:, :1]
        gain_half = gain_ref[0:1, own_half]
        x = xall[0, m, c, own_rows].astype(F32)
        g = xall[1, m, c, own_rows].astype(F32)
        normed = nrm[m, c, own_rows]
        along = (sv + col(dlogits * logits)) * (1.0 / D)
        dinput = inv * (dnormed * gain_half - x * (inv * along))
        actb[1, c, m] = (g + dinput).astype(BF)

        @pl.when(me_l > 0)
        def _():
            gather_there(1, m, me_l - 1)

        send(actb.at[1, c, m], actb.at[1, c, m], ac_s.at[1, m], ac_r.at[1, m], partner)
        racc[0:NE] = racc[0:NE] + dot(dl_hi, normed, TN) + dot(dl_lo, normed, TN)
        racc[NE:NE + 8] = racc[NE:NE + 8] + jnp.broadcast_to(
            jnp.sum(dnormed * x * inv, axis=0, keepdims=True), (8, H)
        )

    def place(k):
        backward = last * (k % 2) + (1 - last) * (k // NM)
        return backward, last * (k // 2) + (1 - last) * (k % NM)

    def step(k, carry):
        backward, m = place(k)
        before, n = place((k + 2 * NM - 1) % (2 * NM))

        @pl.when(backward == 0)
        def _():
            arrive(0, m)
            forward_compute(m)

        @pl.when(backward == 1)
        def _():
            arrive(1, m)
            backward_compute(m)

        late = (k > 0) & ((last == 1) | (k != NM))

        @pl.when(late & (before == 0))
        def _():
            forward_result(n)

        @pl.when(late & (before == 1))
        def _():
            backward_result(n)

        @pl.when(backward == 0)
        def _():
            forward_scatter(m)

        @pl.when(backward == 1)
        def _():
            backward_scatter(m)

        @pl.when((last == 0) & (k == NM - 1))
        def _():
            forward_result(NM - 1)

        return carry

    lax.fori_loop(0, 2 * NM, step, 0)
    backward_result(NM - 1)

    rgs[...] = racc[...]
    mine = c == me_y // (ND // 2)
    for j in range(ND // 2):
        yy = c * (ND // 2) + j
        src = rgs.at[:, pl.ds(j * DS, DS)]

        @pl.when(yy != me_y)
        def _():
            send(src, ybuf.at[me_y], r1_s.at[j], r1_r, {"dp": yy})

        @pl.when(yy == me_y)
        def _():
            copy(src, ybuf.at[me_y], r1_r)

    per = DS // NE

    @pl.when(mine)
    def _():
        wait(ybuf, r1_r)
        total = ybuf[0]
        for j in range(1, ND):
            total = total + ybuf[j]
        ysum[...] = total
        for k in range(NZ):
            for cc in range(2):
                ee = 2 * ((z + k) % NZ) + (c + cc) % 2
                src = ysum.at[:, pl.ds(pl.multiple_of(ee * per // 128 * 128, 128), 128)]
                if k == 0 and cc == 0:
                    copy(src, zbuf.at[z], r2_r)
                else:
                    send(src, zbuf.at[z], r2_s, r2_r, {"expert": ee})

    for m in range(NM):
        for i, ref in enumerate((hid, nsl, dga, dup, gsl)):
            if i in (1, 4):
                wait(ref.at[:, m], y_r.at[i, m])
            else:
                wait(ref.at[pl.ds(0, ND - 1), m], y_r.at[i, m])
    rows = ND * NM * R
    n_t = nsl[...].reshape(rows, DS)
    gg_ref[...] = dot(n_t, dga[...].reshape(rows, F), TN).astype(BF)
    ug_ref[...] = dot(n_t, dup[...].reshape(rows, F), TN).astype(BF)
    dg_ref[...] = dot(hid[...].reshape(rows, F), gsl[...].reshape(rows, DS), TN).astype(BF)

    wait(zbuf, r2_r)
    total = zbuf[0]
    for k in range(1, NZ):
        total = total + zbuf[k]
    rg_ref[...] = total

    for kind, out in enumerate((act_ref, igr_ref)):
        for m in range(NM):
            wait(actb.at[kind, oc, m], ac_r.at[kind, m])
            for half in range(2):
                v = actb[kind, half, m].astype(F32)
                v = v[:8] * mine0 + v[8:] * (1.0 - mine0)
                out[m, :, half * H:(half + 1) * H] = v.astype(BF)

    for kind in range(2):
        wait(ebr.at[kind], e_s.at[kind])
        for m in range(NM):
            wait(xall.at[kind, m, 0], fw_s.at[kind, m])
            wait(actb.at[kind, 0, m], ac_s.at[kind, m])
            sends = me_l < NP - 1 if kind == 0 else me_l > 0
            first = me_l == 0 if kind == 0 else last == 1

            @pl.when(sends)
            def _():
                wait(xall.at[kind, m, 0], ag_s.at[kind, m])

            @pl.when(first)
            def _():
                wait(xall.at[kind, m, 0, pl.ds(0, R - 16)], ag0_s.at[kind, m])

            p, r = ((ps_f, rf), (ps_b, rb))[kind]
            wait(p.at[m], pr_s.at[kind, m])
            wait(r.at[m, pl.ds(0, NZ - 1)], rs_s.at[kind, m])
    wait(pmall.at[pl.ds(0, NE - 1)], m_s)
    for m in range(NM):
        for i, ref in enumerate((hid, nsl, dga, dup, gsl)):
            wait(ref.at[pl.ds(0, ND - 1), m], y_s.at[i, m])
    for j in range(ND // 2):
        @pl.when(c * (ND // 2) + j != me_y)
        def _():
            wait(ybuf.at[0], r1_s.at[j])

    @pl.when(mine)
    def _():
        wait(zbuf, r2_s)
        wait(zbuf.at[pl.ds(0, NZ - 1)], r2_s)


def local(embedded, out_grad, norm_gain, router_weight, gate_weight, up_weight, down_weight, routing):
    NM, _, D = embedded.shape
    F = gate_weight.shape[-1]
    NE, ND, NP = lax.axis_size("expert"), lax.axis_size("dp"), lax.axis_size("pipe")
    NZ, H, R, DS = NE // 2, D // 2, NE * 8, D // ND
    HX = H + 128
    V = pl.BlockSpec(memory_space=pltpu.VMEM)
    A = pl.BlockSpec(memory_space=pl.ANY)

    def vm(*shape):
        return pltpu.VMEM(shape, BF)

    def vf(*shape):
        return pltpu.VMEM(shape, F32)

    sem = pltpu.SemaphoreType.DMA
    shape = jax.ShapeDtypeStruct
    act, igr, gg, ug, dg, rg = pl.pallas_call(
        functools.partial(kernel, (NM, D, F, NE, ND, NP)),
        name="moe_layers",
        in_specs=[V, V, V, V, V, A, A, A],
        out_specs=[V] * 6,
        out_shape=[
            shape((NM, 8, D), BF), shape((NM, 8, D), BF), shape((DS, F), BF), shape((DS, F), BF),
            shape((F, DS), BF), shape((NE + 8, 128), F32),
        ],
        scratch_shapes=[
            vm(D, F), vm(D, F), vm(F, D),
            vm(2, 2, NM, 16, H), vm(2, NM, 16, H), vm(2, NM, 16, H),
            vf(NE, NM, 8, 128),
            vm(2, NM, 2, R, H), vm(NM, 2, R, H),
            vf(NM, R, F), vf(NM, R, F), vm(NM, R, F),
            vf(NM, R, 128), vf(NM, R, 128), vf(NM, R, NE),
            vm(NM, R, H), vm(NM, R, H), vm(NM, R, HX), vm(NM, R, HX),
            vf(R, H), vf(R, HX), vm(NM, R, H), vm(NM, R, HX),
            vm(NM, NZ, 16, H), vm(NM, NZ, 16, HX), vm(2, 2, NM, 16, H),
            vm(ND, NM, R, DS), vm(ND, NM, R, DS), vm(ND, NM, R, F), vm(ND, NM, R, F), vm(ND, NM, R, F),
            vf(NE + 8, H), vf(NE + 8, H), vf(ND, NE + 8, DS), vf(NE + 8, DS), vf(NZ, NE + 8, 128),
            sem((3,)), sem((2,)), sem((2,)), sem, sem,
            sem((2, NM)), sem((2, NM)), sem((2, NM)), sem((2, NM)), sem((2, NM)),
            sem((2, NM)), sem((2, NM)), sem((2, NM)), sem((2, NM)), sem((2, NM)), sem((2, NM)),
            sem((5, NM)), sem((5, NM)), sem((ND // 2,)), sem, sem, sem,
        ],
        compiler_params=pltpu.CompilerParams(
            collective_id=0, has_side_effects=True, vmem_limit_bytes=58 * 2**20
        ),
    )(
        embedded, out_grad, routing[0], norm_gain, router_weight[0],
        gate_weight[0, 0], up_weight[0, 0], down_weight[0, 0],
    )
    per = DS // NE
    part = lax.dynamic_slice_in_dim(rg, lax.axis_index("expert") * per % 128, per, 1)
    return (
        act[None], igr[None], gg[None, None], ug[None, None], dg[None, None],
        part[:NE].T[None], part[NE][None],
    )


def solution(mesh):
    return jax.shard_map(
        local,
        mesh=mesh,
        in_specs=(
            P(None, ("dp", "expert"), None),
            P(None, ("dp", "expert"), None),
            P("pipe", None),
            P("pipe", None, None),
            P("pipe", "expert", None, None),
            P("pipe", "expert", None, None),
            P("pipe", "expert", None, None),
            P("pipe", None, ("dp", "expert"), None),
        ),
        out_specs=(
            P("pipe", None, ("dp", "expert"), None),
            P("pipe", None, ("dp", "expert"), None),
            P("pipe", "expert", "dp", None),
            P("pipe", "expert", "dp", None),
            P("pipe", "expert", None, "dp"),
            P("pipe", ("dp", "expert"), None),
            P("pipe", ("dp", "expert")),
        ),
        check_vma=False,
    )
```

time: 1010 us -> 317 us (0.31); the launches traced: 990 us -> 317 us
  waiting for transfers between devices: 348 us -> 0 us
  Pallas kernels: 0 us -> 304 us
  other arithmetic: 160 us -> 0 us
  blocking collectives: 134 us -> 0 us
  starting transfers between devices: 131 us -> 0 us
  matrix products: 120 us -> 0 us
  local copies, waits for them, and re-layouts: 80.8 us -> 12.6 us
  between operations: 16.1 us -> 0.67 us
    pallas_call x0 -> x1, Pallas kernels: none -> 304 us  [local(): pl.pallas_call(functools.partial(kernel, (NM, D, F, NE, ND, NP)), name='m...]
    all_to_all x24 -> x0, waiting for transfers between devices: 236 us -> none  [the longest x6 68.4 us: local(): lax.all_to_all(sent_grad.reshape(expert_count, CAP, model_width), 'expert...]
    unnamed x1 -> x0, blocking collectives: 134 us -> none
    dot_general x75 -> x0, matrix products: 120 us -> none  [the longest x3 11.6 us: expert_backward(): jnp.einsum('rd,fd->rf', rows_grad, down_map, preferred_element_type=jnp.f...]
    all_to_all x24 -> x0, starting transfers between devices: 105 us -> none  [the longest x6 31.3 us: local(): lax.all_to_all(outgoing.reshape(expert_count, CAP, model_width), 'expert'...]
    unnamed x5 -> x0, waiting for transfers between devices: 74.8 us -> none
    dynamic_update_slice x60 -> x0, other arithmetic: 67.5 us -> none  [store_micro(): lax.dynamic_update_index_in_dim(stored, jnp.where(is_valid, fresh, previo...]
    reduce_sum x50 -> x0, other arithmetic: 37.8 us -> none  [the longest x7 8.48 us: slot_table(): slot_place = flat_ids * CAP + jnp.sum(earlier * member, axis=1)]
  transfers between devices with their start and end apart: 38 -> 0, of which waited for: 30 -> 0; matrix products, arithmetic and copies ran while one was open for 22% -> 0% of each run, Pallas kernels for 0% -> 0%
where the time goes in v1:
time: 317 us
  Pallas kernels  304 us (96%)
  local copies, waits for them, and re-layouts  12.6 us (4%)
    pallas_call x1, Pallas kernels, local(): pl.pallas_call(functools.partial(kernel, (NM, D, F, NE, ND, NP)), name='m...  304 us
    unnamed x8, local copies, waits for them, and re-layouts  9.93 us

profile of v1, /device:TPU:1, one launch (start us, length us, event | category | flops | bytes accessed | tf_op | source)
XLA Modules:
  0.0 317.0 jit_solution(10953788474970882593)
XLA Ops:
  0.6 1.8 copy.15
  2.5 303.7 %moe_layers.1 = (bf16[3,8,2048]{2,1,0:T(8,128)(2,1)}, bf16[3,8,2048]{2,1,0:T(8,128)(2,1)}, bf16[512,768]{1,0:T(8,128)(2,1)}, bf16[512,768]{1,0:T(8,128)(2,1)}, b...) custom-call(bf16[3,8,2048]{2,1,0:T(8,128)(2,1)} %emb_ref.1, bf16[3,8,2048]{2,1,0:T(8,128)(2,1)} %og_ref.1, ...), custom_call_target="tpu_custom_call" | custom-call | tf_op jit(solution)/shard_map/moe_layers/pallas_call | solution.py:455
  306.2 0.0 copy-start
  306.2 1.3 dynamic-slice.1
  307.5 1.4 dynamic-slice_bitcast_fusion
  308.9 1.5 copy.21
  310.4 1.5 copy.22
  312.0 2.1 copy.23
  314.0 2.1 copy.24
  316.1 0.0 copy-done
  316.1 0.9 copy.25
Async XLA Ops:
  306.2 9.9 %copy-start = (bf16[768,512]{1,0:T(8,128)(2,1)S(1)}, bf16[768,512]{1,0:T(8,128)(2,1)}, u32[]{:S(2)}) copy-start(bf16[768,512]{1,0:T(8,128)(2,1)} %get-tuple-element.17) | copy-start | bytes 2359300

commit v2 on v1

--- a/solution.py
+++ b/solution.py
@@ -48,6 +48,7 @@
     own_half = pl.ds(pl.multiple_of(c * H, H), H)
     other_half = pl.ds(pl.multiple_of(oc * H, H), H)
     last = (me_l + 1) // NP
+    far_first = sorted(range(1, NZ), key=lambda k: (-min(k, NZ - k), k))
 
     def send(src, dst, ss, rs, dev):
         pltpu.make_async_remote_copy(
@@ -109,12 +110,12 @@
     def gather_here(kind, m):
         src = src0.at[kind, m]
         dst = xall.at[kind, m, c, own_rows]
-        for k in range(1, NZ):
+        for k in far_first:
             send(src, dst, ag0_s.at[kind, m], ag_r.at[kind, m], {"expert": 2 * ((z + k) % NZ) + c})
         copy(src, dst, ag_r.at[kind, m])
 
     def gather_there(kind, m, section):
-        for k in range(NZ):
+        for k in far_first + [0]:
             send(
                 actb.at[kind, c, m], xall.at[kind, m, c, own_rows],
                 ag_s.at[kind, m], ag_r.at[kind, m],
@@ -147,10 +148,6 @@
         send(
             xall.at[kind, m, c], xall.at[kind, m, c], fw_s.at[kind, m], fw_r.at[kind, m], partner
         )
-        if kind == 0:
-            @pl.when((me_l == 0) & (m < NM - 1))
-            def _():
-                gather_here(0, m + 1)
         wait(xall.at[kind, m, oc], fw_r.at[kind, m])
 
     lane_e = lax.broadcasted_iota(jnp.int32, (R, NE), 1)
@@ -164,7 +161,7 @@
         n1 = (x1 * inv * gain_ref[0:1, H:]).astype(BF)
         nrm[m, 0] = n0
         nrm[m, 1] = n1
-        logits = dot(n0, rw_ref[:H, :], NN) + dot(n1, rw_ref[H:, :], NN)
+        logits = dot(n0, rw_ref[:, :H], NT) + dot(n1, rw_ref[:, H:], NT)
         named = pmall[:, m].reshape(R, 128)[:, :NE]
         chosen = named * jax.nn.sigmoid(logits)
         w = col(jnp.where(lane_e == me_e, chosen, 0.0)) / col(chosen)
@@ -180,10 +177,10 @@
         hid[me_y, m] = (h.astype(F32) * w).astype(BF)
         ps_f[m] = (dot(h, wd[:, other_half], NN) * w).astype(BF)
         send(ps_f.at[m], pr_f.at[m], pr_s.at[0, m], pr_rs.at[0, m], partner)
-        qo_f[...] = dot(h, wd[:, own_half], NN) * w
+        qo_f[m] = dot(h, wd[:, own_half], NN) * w
 
     def scatter(kind, m, q, r):
-        for k in range(1, NZ):
+        for k in far_first:
             zz = (z + k) % NZ
             send(
                 q.at[m, pl.ds(pl.multiple_of(zz * 16, 16), 16)], r.at[m, z],
@@ -210,8 +207,13 @@
 
     def forward_scatter(m):
         wait(pr_f.at[m], pr_rs.at[0, m])
-        qf[m] = (qo_f[...] + pr_f[m].astype(F32)).astype(BF)
+        qf[m] = (qo_f[m] + pr_f[m].astype(F32)).astype(BF)
         scatter(0, m, qf, rf)
+
+        @pl.when((me_l == 0) & (m < NM - 1))
+        def _():
+            gather_here(0, m + 1)
+
         to_replicas(m, (hid,), nrm.at[m], nsl, 0)
 
     def forward_result(m):
@@ -277,8 +279,8 @@
         dlogits = dchosen * chosen * (1.0 - chosen)
         dl_hi = dlogits.astype(BF)
         dl_lo = (dlogits - dl_hi.astype(F32)).astype(BF)
-        router_half = rw_ref[own_half, :]
-        dnormed = total[:, :H] + dot(dl_hi, router_half, NT) + dot(dl_lo, router_half, NT)
+        router_half = rw_ref[:, own_half]
+        dnormed = total[:, :H] + dot(dl_hi, router_half, NN) + dot(dl_lo, router_half, NN)
         inv = invs[m, own_rows][:, :1]
         gain_half = gain_ref[0:1, own_half]
         x = xall[0, m, c, own_rows].astype(F32)
@@ -298,50 +300,39 @@
             jnp.sum(dnormed * x * inv, axis=0, keepdims=True), (8, H)
         )
 
-    def place(k):
-        backward = last * (k % 2) + (1 - last) * (k // NM)
-        return backward, last * (k // 2) + (1 - last) * (k % NM)
-
     def step(k, carry):
-        backward, m = place(k)
-        before, n = place((k + 2 * NM - 1) % (2 * NM))
-
-        @pl.when(backward == 0)
+        end = k // (2 * NM)
+        back = last * (k % 2) + (1 - last) * (k // NM)
+        m = last * (k // 2) + (1 - last) * (k % NM)
+
+        @pl.when((back == 0) & (end == 0))
         def _():
             arrive(0, m)
             forward_compute(m)
 
-        @pl.when(backward == 1)
+        @pl.when((back == 1) & (end == 0))
         def _():
             arrive(1, m)
             backward_compute(m)
-
-        late = (k > 0) & ((last == 1) | (k != NM))
-
-        @pl.when(late & (before == 0))
-        def _():
+            backward_scatter(m)
+
+        after = (last == 1) & (k > 2 * NM)
+
+        @pl.when(((last == 0) & (back == 0) & (end == 0)) | after)
+        def _():
+            n = m * (1 - last) + (k - 2 * NM - 1) * last
+            forward_scatter(n)
             forward_result(n)
 
-        @pl.when(late & (before == 1))
-        def _():
-            backward_result(n)
-
-        @pl.when(backward == 0)
-        def _():
-            forward_scatter(m)
-
-        @pl.when(backward == 1)
-        def _():
-            backward_scatter(m)
-
-        @pl.when((last == 0) & (k == NM - 1))
-        def _():
-            forward_result(NM - 1)
+        inner = (last == 1) & (back == 0) & (k > 0) & (k <= 2 * NM)
+
+        @pl.when(((last == 0) & (back == 1) & (end == 0)) | inner)
+        def _():
+            backward_result(m - last)
 
         return carry
 
-    lax.fori_loop(0, 2 * NM, step, 0)
-    backward_result(NM - 1)
+    lax.fori_loop(0, 3 * NM + 1, step, 0)
 
     rgs[...] = racc[...]
     mine = c == me_y // (ND // 2)
@@ -469,7 +460,7 @@
             vf(NM, R, F), vf(NM, R, F), vm(NM, R, F),
             vf(NM, R, 128), vf(NM, R, 128), vf(NM, R, NE),
             vm(NM, R, H), vm(NM, R, H), vm(NM, R, HX), vm(NM, R, HX),
-            vf(R, H), vf(R, HX), vm(NM, R, H), vm(NM, R, HX),
+            vf(NM, R, H), vf(R, HX), vm(NM, R, H), vm(NM, R, HX),
             vm(NM, NZ, 16, H), vm(NM, NZ, 16, HX), vm(2, 2, NM, 16, H),
             vm(ND, NM, R, DS), vm(ND, NM, R, DS), vm(ND, NM, R, F), vm(ND, NM, R, F), vm(ND, NM, R, F),
             vf(NE + 8, H), vf(NE + 8, H), vf(ND, NE + 8, DS), vf(NE + 8, DS), vf(NZ, NE + 8, 128),
@@ -482,7 +473,7 @@
             collective_id=0, has_side_effects=True, vmem_limit_bytes=58 * 2**20
         ),
     )(
-        embedded, out_grad, routing[0], norm_gain, router_weight[0],
+        embedded, out_grad, routing[0], norm_gain, router_weight[0].T,
         gate_weight[0, 0], up_weight[0, 0], down_weight[0, 0],
     )
     per = DS // NE

time: 317 us -> 264 us (0.83)
  Pallas kernels: 304 us -> 252 us
    pallas_call x1, Pallas kernels: 304 us -> 252 us  [local(): pl.pallas_call(functools.partial(kernel, (NM, D, F, NE, ND, NP)), name='m...]
    unnamed x8 -> x7, local copies, waits for them, and re-layouts: 9.93 us -> 8.08 us
where the time goes in v2:
time: 264 us
  Pallas kernels  252 us (95%)
  local copies, waits for them, and re-layouts  10.8 us (4%)
    pallas_call x1, Pallas kernels, local(): pl.pallas_call(functools.partial(kernel, (NM, D, F, NE, ND, NP)), name='m...  252 us
    unnamed x7, local copies, waits for them, and re-layouts  8.08 us

profile of v2, /device:TPU:1, one launch (start us, length us, event | category | flops | bytes accessed | tf_op | source)
XLA Modules:
  0.0 263.6 jit_solution(16652347485707659004)
XLA Ops:
  0.7 252.1 %moe_layers.1 = (bf16[3,8,2048]{2,1,0:T(8,128)(2,1)}, bf16[3,8,2048]{2,1,0:T(8,128)(2,1)}, bf16[512,768]{1,0:T(8,128)(2,1)}, bf16[512,768]{1,0:T(8,128)(2,1)}, b...) custom-call(bf16[3,8,2048]{2,1,0:T(8,128)(2,1)} %emb_ref.1, bf16[3,8,2048]{2,1,0:T(8,128)(2,1)} %og_ref.1, ...), custom_call_target="tpu_custom_call" | custom-call | tf_op jit(solution)/shard_map/moe_layers/pallas_call | solution.py:446
  252.8 0.0 copy-start
  252.8 1.3 dynamic-slice.1
  254.1 1.4 dynamic-slice_bitcast_fusion
  255.5 1.5 copy.20
  257.0 1.5 copy.21
  258.6 2.1 copy.22
  260.6 2.1 copy.23
  262.7 0.0 copy-done
  262.7 0.9 copy.24
Async XLA Ops:
  252.8 9.9 %copy-start = (bf16[768,512]{1,0:T(8,128)(2,1)S(1)}, bf16[768,512]{1,0:T(8,128)(2,1)}, u32[]{:S(2)}) copy-start(bf16[768,512]{1,0:T(8,128)(2,1)} %get-tuple-element.17) | copy-start | bytes 2359300

commit v3 on v2

v3 whole, which is shorter than its diff:
```python
import functools

import jax
import jax.numpy as jnp
from jax import lax
from jax.experimental import pallas as pl
from jax.experimental.pallas import tpu as pltpu
from jax.sharding import PartitionSpec as P

EPSILON = 1e-06
MESH = pl.DeviceIdType.MESH
BF = jnp.bfloat16
F32 = jnp.float32
NN = (((1,), (0,)), ((), ()))
NT = (((1,), (1,)), ((), ()))
TN = (((0,), (0,)), ((), ()))


def dot(a, b, dims):
    return lax.dot_general(a, b, dims, preferred_element_type=F32)


def col(value):
    return jnp.sum(value, axis=-1, keepdims=True)


def fold(value):
    half = value.shape[1] // 2
    return jnp.concatenate([value[:, :half], value[:, half:]], axis=0)


def twice(value):
    return jnp.concatenate([value, value], axis=0)


def kernel(
    sizes,
    emb_ref, og_ref, ids_ref, gain_ref, rw_ref, gate_hbm, up_hbm, down_hbm,
    act_ref, igr_ref, gg_ref, ug_ref, dg_ref, rg_ref,
    wg, wu, wd, ebs, src0, pmall, xall, nrm, gfull, gpre, upre, hidb, invs, wst, lgs,
    ps_f, pr_f, ps_b, pr_b, qo_f, qo_b, qf, qb, rf, rb, actb,
    nsl, gsl, hid, dgu, racc, rgs, ybuf, ysum, zbuf,
    w_sem, e_s, e_r, m_s, m_r, ag0_s, ag_s, ag_r, fw_s, fw_r, pr_s, pr_rs, rs_s, rs_r, ac_s, ac_r,
    y_s, y_r, yd_s, yd_r, yf_s, yf_r, r1_s, r1_r, r2_s, r2_r,
):
    NM, D, F, NE, ND, NP = sizes
    NZ, H, Q, R, DS = NE // 2, D // 2, D // 4, NE * 4, D // ND
    QX = Q + 128
    me_y = lax.axis_index("dp")
    me_l = lax.axis_index("pipe")
    me_e = lax.axis_index("expert")
    z = me_e // 2
    c = me_e % 2
    oc = 1 - c
    partner = {"expert": me_e + 1 - 2 * c}
    own_rows = pl.ds(pl.multiple_of(z * 16, 16), 16)
    own_tokens = pl.ds(pl.multiple_of(z * 8, 8), 8)
    own_half = pl.ds(pl.multiple_of(c * H, H), H)
    other_half = pl.ds(pl.multiple_of(oc * H, H), H)
    last = (me_l + 1) // NP
    far_first = sorted(range(1, NZ), key=lambda k: (-min(k, NZ - k), k))
    y_up, y_down = (me_y + 1) % ND, (me_y + ND - 1) % ND

    def send(src, dst, ss, rs, dev):
        pltpu.make_async_remote_copy(
            src_ref=src, dst_ref=dst, send_sem=ss, recv_sem=rs, device_id=dev, device_id_type=MESH
        ).start()

    def copy(src, dst, sem):
        pltpu.make_async_copy(src, dst, sem).start()

    def wait(ref, sem):
        pltpu.make_async_copy(ref, ref, sem).wait()

    copy(gate_hbm, wg, w_sem.at[0])
    copy(up_hbm, wu, w_sem.at[1])
    copy(down_hbm, wd, w_sem.at[2])

    barrier = pltpu.get_barrier_semaphore()

    def hello(dev):
        pl.semaphore_signal(barrier, inc=1, device_id=dev, device_id_type=MESH)

    hello(partner)
    for k in range(1, NZ):
        for cc in range(2):
            hello({"expert": 2 * ((z + k) % NZ) + cc})
    for j in range(1, ND):
        hello({"dp": (me_y + j) % ND})
    for step in (1, NP - 1):
        for k in range(NZ):
            hello({"pipe": (me_l + step) % NP, "expert": 2 * ((z + k) % NZ) + c})

    mine0 = (c == 0).astype(F32)
    for kind, ref in enumerate((emb_ref, og_ref)):
        for m in range(NM):
            v = ref[m].astype(F32)
            low, high = v[:, :H], v[:, H:]
            src0[kind, c, m] = fold(low * mine0 + high * (1.0 - mine0)).astype(BF)
            ebs[kind, m] = fold(high * mine0 + low * (1.0 - mine0)).astype(BF)
    lanes8 = lax.broadcasted_iota(jnp.int32, (8, 128), 1)
    for m in range(NM):
        ids = ids_ref[m]
        table = jnp.zeros((8, 128), F32)
        for k in range(ids.shape[1]):
            table = table + (ids[:, k:k + 1] == lanes8).astype(F32)
        pmall[c * NZ + z, m] = table
    racc[...] = jnp.zeros(racc.shape, F32)

    pl.semaphore_wait(barrier, 1 + 2 * (NZ - 1) + (ND - 1) + 2 * NZ)

    for kind in range(2):
        send(ebs.at[kind], src0.at[kind, c], e_s.at[kind], e_r.at[kind], partner)
    my_table = pmall.at[c * NZ + z]
    send(my_table, my_table, m_s, m_r, partner)
    for k in range(1, NZ):
        for cc in range(2):
            send(my_table, my_table, m_s, m_r, {"expert": 2 * ((z + k) % NZ) + cc})

    def gather_here(kind, m, s):
        src = src0.at[kind, s, m]
        dst = xall.at[kind, m, s, c, own_rows]
        for k in far_first:
            send(
                src, dst, ag0_s.at[kind, m, s], ag_r.at[kind, m, s],
                {"expert": 2 * ((z + k) % NZ) + c},
            )
        copy(src, dst, ag_r.at[kind, m, s])

    def gather_there(kind, m, s, section):
        for k in far_first + [0]:
            send(
                actb.at[kind, c, m, s], xall.at[kind, m, s, c, own_rows],
                ag_s.at[kind, m, s], ag_r.at[kind, m, s],
                {"pipe": section, "expert": 2 * ((z + k) % NZ) + c},
            )

    wait(src0.at[0, oc], e_r.at[0])

    @pl.when(me_l == 0)
    def _():
        for s in range(2):
            gather_here(0, 0, s)

    wait(src0.at[1, oc], e_r.at[1])

    @pl.when(last == 1)
    def _():
        for m in range(NM):
            for s in range(2):
                gather_here(1, m, s)

    wait(pmall.at[pl.ds(0, NE - 1)], m_r)
    wait(wg, w_sem.at[0])
    wait(wu, w_sem.at[1])
    wait(wd, w_sem.at[2])

    def arrive(kind, m, s):
        got = xall.at[kind, m, s, c]
        wait(got, ag_r.at[kind, m, s])
        send(got, got, fw_s.at[kind, m, s], fw_r.at[kind, m, s], partner)
        wait(xall.at[kind, m, s, oc], fw_r.at[kind, m, s])

    def quarters(kind, m, s):
        out = []
        for half in range(2):
            v = xall[kind, m, s, half].astype(F32).reshape(NZ, 2, 8, Q)
            out += [v[:, 0].reshape(R, Q), v[:, 1].reshape(R, Q)]
        return out

    lane_e = lax.broadcasted_iota(jnp.int32, (R, NE), 1)
    lane_x = lax.broadcasted_iota(jnp.int32, (R, 128), 1)

    def forward_compute(m, s):
        xs = quarters(0, m, s)
        square = xs[0] * xs[0]
        for v in xs[1:]:
            square = square + v * v
        inv = lax.rsqrt(col(square) * (1.0 / D) + EPSILON)
        for i, v in enumerate(xs):
            nrm[m, s, :, i * Q:(i + 1) * Q] = (v * inv * gain_ref[0:1, i * Q:(i + 1) * Q]).astype(BF)
        normed = nrm[m, s]
        logits = dot(normed, rw_ref[...], NT)
        named = pmall[s * NZ:(s + 1) * NZ, m].reshape(R, 128)[:, :NE]
        chosen = named * jax.nn.sigmoid(logits)
        w = col(jnp.where(lane_e == me_e, chosen, 0.0)) / col(chosen)
        invs[m, s] = jnp.broadcast_to(inv, (R, 128))
        wst[m, s] = jnp.broadcast_to(w, (R, 128))
        lgs[m, s] = logits
        a = dot(normed, wg[...], NN)
        b = dot(normed, wu[...], NN)
        gpre[m, s] = a
        upre[m, s] = b
        h = (a * jax.nn.sigmoid(a) * b).astype(BF)
        hidb[m, s] = h
        hid[me_y, m, s] = (h.astype(F32) * w).astype(BF)
        ps_f[m, s] = (dot(h, wd[:, other_half], NN) * w).astype(BF)
        send(ps_f.at[m, s], pr_f.at[m, s], pr_s.at[0, m, s], pr_rs.at[0, m, s], partner)
        qo_f[m, s] = dot(h, wd[:, own_half], NN) * w

    def scatter(kind, m, s, q, r):
        for k in far_first:
            zz = (z + k) % NZ
            send(
                q.at[m, s, pl.ds(pl.multiple_of(zz * 16, 16), 16)], r.at[m, s, z],
                rs_s.at[kind, m, s], rs_r.at[kind, m, s], {"expert": 2 * zz + c},
            )
        copy(q.at[m, s, own_rows], r.at[m, s, z], rs_r.at[kind, m, s])

    def part(ref, yy):
        return ref.at[:, pl.ds(pl.multiple_of(yy * DS, DS), DS)]

    def folded(v):
        width = v.shape[1] // 2
        low, high = v[:, :width].reshape(NZ, 1, 8, width), v[:, width:].reshape(NZ, 1, 8, width)
        return jnp.concatenate([low, high], axis=1).reshape(NZ * 16, width)

    def forward_scatter(m, s):
        wait(pr_f.at[m, s], pr_rs.at[0, m, s])
        qf[m, s] = folded(qo_f[m, s] + pr_f[m, s].astype(F32)).astype(BF)
        scatter(0, m, s, qf, rf)

        @pl.when((me_l == 0) & (m < NM - 1))
        def _():
            gather_here(0, m + 1, s)

    def forward_replicas(m, s):
        for j in range(1, ND):
            yy = (me_y + j) % ND
            mine = hid.at[me_y, m, s]
            send(mine, mine, y_s.at[0, m], y_r.at[0, m], {"dp": yy})
            send(part(nrm.at[m, s], yy), nsl.at[me_y, m, s], y_s.at[1, m], y_r.at[1, m], {"dp": yy})
        copy(part(nrm.at[m, s], me_y), nsl.at[me_y, m, s], y_r.at[1, m])

    def keep(kind, m, s):
        block = actb.at[kind, c, m, s]

        @pl.when(oc == s)
        def _():
            send(block, block, ac_s.at[kind, m], ac_r.at[kind, m], partner)

    def forward_result(m, s):
        wait(rf.at[m, s], rs_r.at[0, m, s])
        total = xall[0, m, s, c, own_rows].astype(F32)
        for k in range(NZ):
            total = total + rf[m, s, k].astype(F32)
        actb[0, c, m, s] = total.astype(BF)

        @pl.when(last == 0)
        def _():
            gather_there(0, m, s, me_l + 1)

        keep(0, m, s)

    def backward_compute(m, s):
        for i, v in enumerate(quarters(1, m, s)):
            gfull[m, s, :, i * Q:(i + 1) * Q] = v.astype(BF)
        dh = dot(gfull[m, s], wd[...], NT)
        w = wst[m, s][:, :1]
        a = gpre[m, s]
        b = upre[m, s]
        dw = col(dh * hidb[m, s].astype(F32))
        dhw = dh * w
        sg = jax.nn.sigmoid(a)
        dgate = (dhw * b * sg * (1.0 + a * (1.0 - sg))).astype(BF)
        dupv = (dhw * (a * sg)).astype(BF)
        dgu[me_y, m, s, 0] = dgate
        dgu[me_y, m, s, 1] = dupv
        sv = col(dgate.astype(F32) * a + dupv.astype(F32) * b)
        dw_hi = dw.astype(BF).astype(F32)
        sv_hi = sv.astype(BF).astype(F32)
        ext = jnp.where(lane_x == me_e, dw_hi, 0.0)
        ext = jnp.where(lane_x == NE + me_e, dw - dw_hi, ext)
        ext = jnp.where(lane_x == 2 * NE + me_e, sv_hi, ext)
        ext = jnp.where(lane_x == 3 * NE + me_e, sv - sv_hi, ext)
        ps_b[m, s, :, :H] = (
            dot(dgate, wg[other_half, :], NT) + dot(dupv, wu[other_half, :], NT)
        ).astype(BF)
        ps_b[m, s, :, H:] = ext.astype(BF)
        send(ps_b.at[m, s], pr_b.at[m, s], pr_s.at[1, m, s], pr_rs.at[1, m, s], partner)
        qo_b[:, :H] = dot(dgate, wg[own_half, :], NT) + dot(dupv, wu[own_half, :], NT)
        qo_b[:, H:] = ext

    def backward_scatter(m, s):
        wait(pr_b.at[m, s], pr_rs.at[1, m, s])
        q = qo_b[...] + pr_b[m, s].astype(F32)
        qb[m, s, :, :Q] = folded(q[:, :H]).astype(BF)
        ext = q[:, H:].reshape(NZ, 1, 8, 128)
        qb[m, s, :, Q:] = (
            jnp.concatenate([ext, jnp.zeros_like(ext)], axis=1).reshape(NZ * 16, 128).astype(BF)
        )
        scatter(1, m, s, qb, rb)

    def backward_replicas(m, s):
        mine = dgu.at[me_y, m, s]
        send(mine, mine, yd_s.at[0, m, s], yd_r.at[0, m, s], {"dp": y_up})
        send(mine, mine, yd_s.at[1, m, s], yd_r.at[1, m, s], {"dp": y_down})
        for j in range(1, ND):
            yy = (me_y + j) % ND
            send(part(gfull.at[m, s], yy), gsl.at[me_y, m, s], y_s.at[2, m], y_r.at[2, m], {"dp": yy})
        copy(part(gfull.at[m, s], me_y), gsl.at[me_y, m, s], y_r.at[2, m])

    def pass_on(m):
        for s, source, target in ((0, y_down, y_up), (1, y_up, y_down)):
            block = dgu.at[source, m, s]
            wait(block, yd_r.at[s, m, s])
            send(block, block, yf_s.at[m, s], yf_r.at[m, s], {"dp": target})

    def backward_result(m, s):
        wait(rb.at[m, s], rs_r.at[1, m, s])
        total = rb[m, s, 0].astype(F32)
        for k in range(1, NZ):
            total = total + rb[m, s, k].astype(F32)
        ext = total[:8, Q:]
        dw = ext[:, :NE] + ext[:, NE:2 * NE]
        sv = col(ext[:, 2 * NE:3 * NE] + ext[:, 3 * NE:4 * NE])
        logits = lgs[m, s, own_tokens]
        named = pmall[s * NZ + z, m][:, :NE]
        chosen = named * jax.nn.sigmoid(logits)
        prob_total = col(chosen)
        weights = chosen / prob_total
        dchosen = (dw - col(dw * weights)) / prob_total
        dlogits = dchosen * chosen * (1.0 - chosen)
        dl_hi = dlogits.astype(BF).astype(F32)
        dl = jnp.concatenate([dl_hi, dlogits - dl_hi], axis=0).astype(BF)
        term = dot(dl, rw_ref[:, own_half], NN)
        dnormed = total[:, :Q] + fold(term[:8] + term[8:])
        inv = twice(invs[m, s, own_tokens][:, :1])
        gain_row = gain_ref[0:1, own_half]
        gain = jnp.concatenate(
            [jnp.broadcast_to(gain_row[:, :Q], (8, Q)), jnp.broadcast_to(gain_row[:, Q:], (8, Q))],
            axis=0,
        )
        x = xall[0, m, s, c, own_rows].astype(F32)
        g = xall[1, m, s, c, own_rows].astype(F32)
        along = twice((sv + col(dlogits * logits)) * (1.0 / D))
        dinput = inv * (dnormed * gain - x * (inv * along))
        actb[1, c, m, s] = (g + dinput).astype(BF)

        @pl.when(me_l > 0)
        def _():
            gather_there(1, m, s, me_l - 1)

        keep(1, m, s)
        normed = x * inv * gain
        gained = dnormed * x * inv
        for i in range(2):
            rows = slice(8 * i, 8 * i + 8)
            cols = slice(Q * i, Q * i + Q)
            racc[0:NE, cols] = racc[0:NE, cols] + dot(dl, twice(normed[rows]).astype(BF), TN)
            racc[NE:NE + 8, cols] = racc[NE:NE + 8, cols] + gained[rows]

    def step(k, carry):
        m = k % NM
        first = k < NM
        is_last = last == 1
        forward = (first & (last == 0)) | ((k >= NM) & is_last)
        backward = ((k >= NM) & (last == 0)) | (first & is_last)
        for s in range(2):
            @pl.when(first)
            def _():
                arrive(0, m, s)
                forward_compute(m, s)

            @pl.when(forward)
            def _():
                forward_scatter(m, s)

            @pl.when(backward)
            def _():
                arrive(1, m, s)
                backward_compute(m, s)
                backward_scatter(m, s)
                backward_replicas(m, s)

            @pl.when(first)
            def _():
                forward_replicas(m, s)

        @pl.when(backward & (m > 0))
        def _():
            pass_on(m - 1)

        for s in range(2):
            @pl.when(forward)
            def _():
                forward_result(m, s)

            @pl.when(backward)
            def _():
                backward_result(m, s)

        return carry

    lax.fori_loop(0, 2 * NM, step, 0)
    pass_on(NM - 1)

    rgs[0:NE] = racc[0:NE]
    rgs[NE:NE + 8] = jnp.broadcast_to(
        jnp.sum(racc[NE:NE + 8], axis=0, keepdims=True), (8, H)
    )
    mine = c == me_y // (ND // 2)
    for j in range(ND // 2):
        yy = c * (ND // 2) + j
        src = rgs.at[:, pl.ds(j * DS, DS)]

        @pl.when(yy != me_y)
        def _():
            send(src, ybuf.at[me_y], r1_s.at[j], r1_r, {"dp": yy})

        @pl.when(yy == me_y)
        def _():
            copy(src, ybuf.at[me_y], r1_r)

    per = DS // NE

    @pl.when(mine)
    def _():
        wait(ybuf, r1_r)
        total = ybuf[0]
        for j in range(1, ND):
            total = total + ybuf[j]
        ysum[...] = total
        for k in range(NZ):
            for cc in range(2):
                ee = 2 * ((z + k) % NZ) + (c + cc) % 2
                src = ysum.at[:, pl.ds(pl.multiple_of(ee * per // 128 * 128, 128), 128)]
                if k == 0 and cc == 0:
                    copy(src, zbuf.at[z], r2_r)
                else:
                    send(src, zbuf.at[z], r2_s, r2_r, {"expert": ee})

    far = (me_y + 2) % ND
    for m in range(NM):
        wait(hid.at[pl.ds(0, ND - 1), m], y_r.at[0, m])
        wait(nsl.at[:, m], y_r.at[1, m])
        wait(gsl.at[:, m], y_r.at[2, m])
        for s in range(2):
            wait(dgu.at[y_down, m, s], yd_r.at[1 - s, m, s])
            wait(dgu.at[far, m, s], yf_r.at[m, s])
    rows = ND * NM * 2 * R
    n_t = nsl[...].reshape(rows, DS)
    gg_ref[...] = dot(n_t, dgu[:, :, :, 0].reshape(rows, F), TN).astype(BF)
    ug_ref[...] = dot(n_t, dgu[:, :, :, 1].reshape(rows, F), TN).astype(BF)
    dg_ref[...] = dot(hid[...].reshape(rows, F), gsl[...].reshape(rows, DS), TN).astype(BF)

    wait(zbuf, r2_r)
    total = zbuf[0]
    for k in range(1, NZ):
        total = total + zbuf[k]
    rg_ref[...] = total

    for kind, out in enumerate((act_ref, igr_ref)):
        for m in range(NM):
            wait(actb.at[kind, oc, m, c], ac_r.at[kind, m])
            for half in range(2):
                v = actb[kind, half, m, c].astype(F32)
                out[m, :, half * H:half * H + Q] = v[:8].astype(BF)
                out[m, :, half * H + Q:(half + 1) * H] = v[8:].astype(BF)

    for kind in range(2):
        wait(ebs.at[kind], e_s.at[kind])
        p, r = ((ps_f, rf), (ps_b, rb))[kind]
        sends = me_l < NP - 1 if kind == 0 else me_l > 0
        origin = me_l == 0 if kind == 0 else last == 1
        for m in range(NM):
            wait(actb.at[kind, 0, m, 0], ac_s.at[kind, m])
            for s in range(2):
                wait(xall.at[kind, m, s, 0], fw_s.at[kind, m, s])
                wait(p.at[m, s], pr_s.at[kind, m, s])
                wait(r.at[m, s, pl.ds(0, NZ - 1)], rs_s.at[kind, m, s])

                @pl.when(sends)
                def _():
                    wait(xall.at[kind, m, s, 0], ag_s.at[kind, m, s])

                @pl.when(origin)
                def _():
                    wait(xall.at[kind, m, s, 0, pl.ds(0, 16 * NZ - 16)], ag0_s.at[kind, m, s])

    wait(pmall.at[pl.ds(0, NE - 1)], m_s)
    for m in range(NM):
        for i, ref in enumerate((hid, nsl, gsl)):
            wait(ref.at[pl.ds(0, ND - 1), m], y_s.at[i, m])
        for s in range(2):
            wait(dgu.at[0, m, s], yd_s.at[0, m, s])
            wait(dgu.at[0, m, s], yd_s.at[1, m, s])
            wait(dgu.at[0, m, s], yf_s.at[m, s])
    for j in range(ND // 2):
        @pl.when(c * (ND // 2) + j != me_y)
        def _():
            wait(ybuf.at[0], r1_s.at[j])

    @pl.when(mine)
    def _():
        wait(zbuf, r2_s)
        wait(zbuf.at[pl.ds(0, NZ - 1)], r2_s)


def local(embedded, out_grad, norm_gain, router_weight, gate_weight, up_weight, down_weight, routing):
    NM, _, D = embedded.shape
    F = gate_weight.shape[-1]
    NE, ND, NP = lax.axis_size("expert"), lax.axis_size("dp"), lax.axis_size("pipe")
    NZ, H, Q, R, DS = NE // 2, D // 2, D // 4, NE * 4, D // ND
    QX = Q + 128
    V = pl.BlockSpec(memory_space=pltpu.VMEM)
    A = pl.BlockSpec(memory_space=pl.ANY)

    def vm(*shape):
        return pltpu.VMEM(shape, BF)

    def vf(*shape):
        return pltpu.VMEM(shape, F32)

    sem = pltpu.SemaphoreType.DMA
    unit = sem((2, NM, 2))
    shape = jax.ShapeDtypeStruct
    act, igr, gg, ug, dg, rg = pl.pallas_call(
        functools.partial(kernel, (NM, D, F, NE, ND, NP)),
        name="moe_layers",
        in_specs=[V, V, V, V, V, A, A, A],
        out_specs=[V] * 6,
        out_shape=[
            shape((NM, 8, D), BF), shape((NM, 8, D), BF), shape((DS, F), BF), shape((DS, F), BF),
            shape((F, DS), BF), shape((NE + 8, 128), F32),
        ],
        scratch_shapes=[
            vm(D, F), vm(D, F), vm(F, D),
            vm(2, NM, 16, Q), vm(2, 2, NM, 16, Q),
            vf(NE, NM, 8, 128),
            vm(2, NM, 2, 2, NZ * 16, Q), vm(NM, 2, R, D), vm(NM, 2, R, D),
            vf(NM, 2, R, F), vf(NM, 2, R, F), vm(NM, 2, R, F),
            vf(NM, 2, R, 128), vf(NM, 2, R, 128), vf(NM, 2, R, NE),
            vm(NM, 2, R, H), vm(NM, 2, R, H), vm(NM, 2, R, H + 128), vm(NM, 2, R, H + 128),
            vf(NM, 2, R, H), vf(R, H + 128), vm(NM, 2, NZ * 16, Q), vm(NM, 2, NZ * 16, QX),
            vm(NM, 2, NZ, 16, Q), vm(NM, 2, NZ, 16, QX), vm(2, 2, NM, 2, 16, Q),
            vm(ND, NM, 2, R, DS), vm(ND, NM, 2, R, DS), vm(ND, NM, 2, R, F), vm(ND, NM, 2, 2, R, F),
            vf(NE + 8, H), vf(NE + 8, H), vf(ND, NE + 8, DS), vf(NE + 8, DS), vf(NZ, NE + 8, 128),
            sem((3,)), sem((2,)), sem((2,)), sem, sem,
            unit, unit, unit, unit, unit, unit, unit, unit, unit, sem((2, NM)), sem((2, NM)),
            sem((3, NM)), sem((3, NM)), unit, unit, sem((NM, 2)), sem((NM, 2)),
            sem((ND // 2,)), sem, sem, sem,
        ],
        compiler_params=pltpu.CompilerParams(
            collective_id=0, has_side_effects=True, vmem_limit_bytes=58 * 2**20
        ),
    )(
        embedded, out_grad, routing[0], norm_gain, router_weight[0].T,
        gate_weight[0, 0], up_weight[0, 0], down_weight[0, 0],
    )
    per = DS // NE
    part = lax.dynamic_slice_in_dim(rg, lax.axis_index("expert") * per % 128, per, 1)
    return (
        act[None], igr[None], gg[None, None], ug[None, None], dg[None, None],
        part[:NE].T[None], part[NE][None],
    )


def solution(mesh):
    return jax.shard_map(
        local,
        mesh=mesh,
        in_specs=(
            P(None, ("dp", "expert"), None),
            P(None, ("dp", "expert"), None),
            P("pipe", None),
            P("pipe", None, None),
            P("pipe", "expert", None, None),
            P("pipe", "expert", None, None),
            P("pipe", "expert", None, None),
            P("pipe", None, ("dp", "expert"), None),
        ),
        out_specs=(
            P("pipe", None, ("dp", "expert"), None),
            P("pipe", None, ("dp", "expert"), None),
            P("pipe", "expert", "dp", None),
            P("pipe", "expert", "dp", None),
            P("pipe", "expert", None, "dp"),
            P("pipe", ("dp", "expert"), None),
            P("pipe", ("dp", "expert")),
        ),
        check_vma=False,
    )
```

time: 264 us -> 246 us (0.932)
  Pallas kernels: 252 us -> 234 us
    pallas_call x1, Pallas kernels: 252 us -> 234 us  [local(): pl.pallas_call(functools.partial(kernel, (NM, D, F, NE, ND, NP)), name='m...]
where the time goes in v3:
time: 246 us
  Pallas kernels  234 us (95%)
  local copies, waits for them, and re-layouts  10.8 us (4%)
    pallas_call x1, Pallas kernels, local(): pl.pallas_call(functools.partial(kernel, (NM, D, F, NE, ND, NP)), name='m...  234 us
    unnamed x7, local copies, waits for them, and re-layouts  8.08 us

profile of v3, /device:TPU:1, one launch (start us, length us, event | category | flops | bytes accessed | tf_op | source)
XLA Modules:
  0.0 245.8 jit_solution(9157040597252692824)
XLA Ops:
  0.7 234.4 %moe_layers.1 = (bf16[3,8,2048]{2,1,0:T(8,128)(2,1)}, bf16[3,8,2048]{2,1,0:T(8,128)(2,1)}, bf16[512,768]{1,0:T(8,128)(2,1)}, bf16[512,768]{1,0:T(8,128)(2,1)}, b...) custom-call(bf16[3,8,2048]{2,1,0:T(8,128)(2,1)} %emb_ref.1, bf16[3,8,2048]{2,1,0:T(8,128)(2,1)} %og_ref.1, ...), custom_call_target="tpu_custom_call" | custom-call | tf_op jit(solution)/shard_map/moe_layers/pallas_call | solution.py:518
  235.0 0.0 copy-start
  235.0 1.3 dynamic-slice.1
  236.4 1.4 dynamic-slice_bitcast_fusion
  237.7 1.5 copy.20
  239.3 1.5 copy.21
  240.8 2.1 copy.22
  242.9 2.1 copy.23
  244.9 0.0 copy-done
  244.9 0.9 copy.24
Async XLA Ops:
  235.0 9.9 %copy-start = (bf16[768,512]{1,0:T(8,128)(2,1)S(1)}, bf16[768,512]{1,0:T(8,128)(2,1)}, u32[]{:S(2)}) copy-start(bf16[768,512]{1,0:T(8,128)(2,1)} %get-tuple-element.17) | copy-start | bytes 2359300

commit v4 on v3

--- a/solution.py
+++ b/solution.py
@@ -33,11 +33,25 @@
     return jnp.concatenate([value, value], axis=0)
 
 
+def hand_over(*refs):
+    sems = refs[21]
+    count = range(7)
+    come = [pltpu.make_async_copy(refs[i], refs[14 + i], sems.at[0, i]) for i in count]
+    go = [pltpu.make_async_copy(refs[14 + i], refs[7 + i], sems.at[1, i]) for i in count]
+    for move in come:
+        move.start()
+    for i in count:
+        come[i].wait()
+        go[i].start()
+    for move in go:
+        move.wait()
+
+
 def kernel(
     sizes,
     emb_ref, og_ref, ids_ref, gain_ref, rw_ref, gate_hbm, up_hbm, down_hbm,
-    act_ref, igr_ref, gg_ref, ug_ref, dg_ref, rg_ref,
-    wg, wu, wd, ebs, src0, pmall, xall, nrm, gfull, gpre, upre, hidb, invs, wst, lgs,
+    act_ref, igr_ref, gg_ref, ug_ref, dg_ref, rt_ref, gn_ref,
+    wg, wu, wd, wgt, wut, wdt, ebs, src0, pmall, xall, nrm, gfull, gpre, upre, hidb, invs, wst, lgs,
     ps_f, pr_f, ps_b, pr_b, qo_f, qo_b, qf, qb, rf, rb, actb,
     nsl, gsl, hid, dgu, racc, rgs, ybuf, ysum, zbuf,
     w_sem, e_s, e_r, m_s, m_r, ag0_s, ag_s, ag_r, fw_s, fw_r, pr_s, pr_rs, rs_s, rs_r, ac_s, ac_r,
@@ -117,49 +131,43 @@
         for cc in range(2):
             send(my_table, my_table, m_s, m_r, {"expert": 2 * ((z + k) % NZ) + cc})
 
-    def gather_here(kind, m, s):
-        src = src0.at[kind, s, m]
-        dst = xall.at[kind, m, s, c, own_rows]
-        for k in far_first:
-            send(
-                src, dst, ag0_s.at[kind, m, s], ag_r.at[kind, m, s],
-                {"expert": 2 * ((z + k) % NZ) + c},
-            )
-        copy(src, dst, ag_r.at[kind, m, s])
-
-    def gather_there(kind, m, s, section):
+    def gather(kind, m, s, src, sems, section):
         for k in far_first + [0]:
             send(
-                actb.at[kind, c, m, s], xall.at[kind, m, s, c, own_rows],
-                ag_s.at[kind, m, s], ag_r.at[kind, m, s],
+                src, xall.at[kind, m, s, c, own_rows], sems.at[kind, m, s], ag_r.at[kind, m, s],
                 {"pipe": section, "expert": 2 * ((z + k) % NZ) + c},
             )
 
-    wait(src0.at[0, oc], e_r.at[0])
-
-    @pl.when(me_l == 0)
-    def _():
-        for s in range(2):
-            gather_here(0, 0, s)
-
-    wait(src0.at[1, oc], e_r.at[1])
-
-    @pl.when(last == 1)
-    def _():
-        for m in range(NM):
-            for s in range(2):
-                gather_here(1, m, s)
+    for kind in range(2):
+        wait(src0.at[kind, oc], e_r.at[kind])
+
+        @pl.when(me_l == NP - 1 - kind)
+        def _():
+            for m in range(NM):
+                for s in range(2):
+                    gather(kind, m, s, src0.at[kind, s, m], ag0_s, (NP - 1) * kind)
 
     wait(pmall.at[pl.ds(0, NE - 1)], m_r)
     wait(wg, w_sem.at[0])
     wait(wu, w_sem.at[1])
     wait(wd, w_sem.at[2])
+    for j in range(D // 256):
+        rows = slice(256 * j, 256 * j + 256)
+        wgt[:, rows] = wg[rows, :].T
+        wut[:, rows] = wu[rows, :].T
+        wdt[rows, :] = wd[:, rows].T
 
     def arrive(kind, m, s):
         got = xall.at[kind, m, s, c]
         wait(got, ag_r.at[kind, m, s])
         send(got, got, fw_s.at[kind, m, s], fw_r.at[kind, m, s], partner)
         wait(xall.at[kind, m, s, oc], fw_r.at[kind, m, s])
+
+    @pl.when(last == 1)
+    def _():
+        for m in range(NM):
+            for s in range(2):
+                arrive(1, m, s)
 
     def quarters(kind, m, s):
         out = []
@@ -181,7 +189,7 @@
             nrm[m, s, :, i * Q:(i + 1) * Q] = (v * inv * gain_ref[0:1, i * Q:(i + 1) * Q]).astype(BF)
         normed = nrm[m, s]
         logits = dot(normed, rw_ref[...], NT)
-        named = pmall[s * NZ:(s + 1) * NZ, m].reshape(R, 128)[:, :NE]
+        named = pmall[pl.ds(s * NZ, NZ), m].reshape(R, 128)[:, :NE]
         chosen = named * jax.nn.sigmoid(logits)
         w = col(jnp.where(lane_e == me_e, chosen, 0.0)) / col(chosen)
         invs[m, s] = jnp.broadcast_to(inv, (R, 128))
@@ -220,10 +228,6 @@
         qf[m, s] = folded(qo_f[m, s] + pr_f[m, s].astype(F32)).astype(BF)
         scatter(0, m, s, qf, rf)
 
-        @pl.when((me_l == 0) & (m < NM - 1))
-        def _():
-            gather_here(0, m + 1, s)
-
     def forward_replicas(m, s):
         for j in range(1, ND):
             yy = (me_y + j) % ND
@@ -248,14 +252,14 @@
 
         @pl.when(last == 0)
         def _():
-            gather_there(0, m, s, me_l + 1)
+            gather(0, m, s, actb.at[0, c, m, s], ag_s, me_l + 1)
 
         keep(0, m, s)
 
     def backward_compute(m, s):
         for i, v in enumerate(quarters(1, m, s)):
             gfull[m, s, :, i * Q:(i + 1) * Q] = v.astype(BF)
-        dh = dot(gfull[m, s], wd[...], NT)
+        dh = dot(gfull[m, s], wdt[...], NN)
         w = wst[m, s][:, :1]
         a = gpre[m, s]
         b = upre[m, s]
@@ -274,11 +278,11 @@
         ext = jnp.where(lane_x == 2 * NE + me_e, sv_hi, ext)
         ext = jnp.where(lane_x == 3 * NE + me_e, sv - sv_hi, ext)
         ps_b[m, s, :, :H] = (
-            dot(dgate, wg[other_half, :], NT) + dot(dupv, wu[other_half, :], NT)
+            dot(dgate, wgt[:, other_half], NN) + dot(dupv, wut[:, other_half], NN)
         ).astype(BF)
         ps_b[m, s, :, H:] = ext.astype(BF)
         send(ps_b.at[m, s], pr_b.at[m, s], pr_s.at[1, m, s], pr_rs.at[1, m, s], partner)
-        qo_b[:, :H] = dot(dgate, wg[own_half, :], NT) + dot(dupv, wu[own_half, :], NT)
+        qo_b[:, :H] = dot(dgate, wgt[:, own_half], NN) + dot(dupv, wut[:, own_half], NN)
         qo_b[:, H:] = ext
 
     def backward_scatter(m, s):
@@ -339,7 +343,7 @@
 
         @pl.when(me_l > 0)
         def _():
-            gather_there(1, m, s, me_l - 1)
+            gather(1, m, s, actb.at[1, c, m, s], ag_s, me_l - 1)
 
         keep(1, m, s)
         normed = x * inv * gain
@@ -350,49 +354,64 @@
             racc[0:NE, cols] = racc[0:NE, cols] + dot(dl, twice(normed[rows]).astype(BF), TN)
             racc[NE:NE + 8, cols] = racc[NE:NE + 8, cols] + gained[rows]
 
+    units = 2 * NM
+
     def step(k, carry):
-        m = k % NM
-        first = k < NM
+        u = k % units
+        m, s = u // 2, u % 2
+        before = (u + units - 1) % units
+        bm, bs = before // 2, before % 2
+        first = k < units
         is_last = last == 1
-        forward = (first & (last == 0)) | ((k >= NM) & is_last)
-        backward = ((k >= NM) & (last == 0)) | (first & is_last)
-        for s in range(2):
-            @pl.when(first)
-            def _():
-                arrive(0, m, s)
-                forward_compute(m, s)
-
-            @pl.when(forward)
-            def _():
-                forward_scatter(m, s)
-
-            @pl.when(backward)
-            def _():
-                arrive(1, m, s)
-                backward_compute(m, s)
-                backward_scatter(m, s)
-                backward_replicas(m, s)
-
-            @pl.when(first)
-            def _():
-                forward_replicas(m, s)
-
-        @pl.when(backward & (m > 0))
+        forward = (first & (last == 0)) | ((k >= units) & is_last)
+        backward = ((k >= units) & (last == 0)) | (first & is_last)
+
+        @pl.when(first)
+        def _():
+            arrive(0, m, s)
+            forward_compute(m, s)
+
+        @pl.when(backward & (last == 0))
+        def _():
+            arrive(1, m, s)
+
+        @pl.when(backward)
+        def _():
+            backward_compute(m, s)
+
+        @pl.when(forward & (u > 0))
+        def _():
+            forward_result(bm, bs)
+
+        @pl.when(backward & (u > 0))
+        def _():
+            backward_result(bm, bs)
+
+        @pl.when(forward)
+        def _():
+            forward_scatter(m, s)
+            forward_replicas(m, s)
+
+        @pl.when(backward)
+        def _():
+            backward_scatter(m, s)
+            backward_replicas(m, s)
+
+        @pl.when(backward & (s == 1) & (m > 0))
         def _():
             pass_on(m - 1)
 
-        for s in range(2):
-            @pl.when(forward)
-            def _():
-                forward_result(m, s)
-
-            @pl.when(backward)
-            def _():
-                backward_result(m, s)
+        @pl.when(forward & (u == units - 1))
+        def _():
+            forward_result(m, s)
+
+        @pl.when(backward & (u == units - 1))
+        def _():
+            backward_result(m, s)
 
         return carry
 
-    lax.fori_loop(0, 2 * NM, step, 0)
+    lax.fori_loop(0, 2 * units, step, 0)
     pass_on(NM - 1)
 
     rgs[0:NE] = racc[0:NE]
@@ -411,6 +430,14 @@
         @pl.when(yy == me_y)
         def _():
             copy(src, ybuf.at[me_y], r1_r)
+
+    far = (me_y + 2) % ND
+    rows = ND * NM * 2 * R
+    for m in range(NM):
+        wait(hid.at[pl.ds(0, ND - 1), m], y_r.at[0, m])
+        wait(nsl.at[:, m], y_r.at[1, m])
+        wait(gsl.at[:, m], y_r.at[2, m])
+    dg_ref[...] = dot(hid[...].reshape(rows, F), gsl[...].reshape(rows, DS), TN).astype(BF)
 
     per = DS // NE
 
@@ -430,25 +457,25 @@
                 else:
                     send(src, zbuf.at[z], r2_s, r2_r, {"expert": ee})
 
-    far = (me_y + 2) % ND
     for m in range(NM):
-        wait(hid.at[pl.ds(0, ND - 1), m], y_r.at[0, m])
-        wait(nsl.at[:, m], y_r.at[1, m])
-        wait(gsl.at[:, m], y_r.at[2, m])
         for s in range(2):
             wait(dgu.at[y_down, m, s], yd_r.at[1 - s, m, s])
             wait(dgu.at[far, m, s], yf_r.at[m, s])
-    rows = ND * NM * 2 * R
     n_t = nsl[...].reshape(rows, DS)
     gg_ref[...] = dot(n_t, dgu[:, :, :, 0].reshape(rows, F), TN).astype(BF)
     ug_ref[...] = dot(n_t, dgu[:, :, :, 1].reshape(rows, F), TN).astype(BF)
-    dg_ref[...] = dot(hid[...].reshape(rows, F), gsl[...].reshape(rows, DS), TN).astype(BF)
 
     wait(zbuf, r2_r)
     total = zbuf[0]
     for k in range(1, NZ):
         total = total + zbuf[k]
-    rg_ref[...] = total
+    picked = jnp.zeros((NE + 8, per), F32)
+    for i in range(128 // per):
+        picked = jnp.where(
+            lax.rem(me_e, 128 // per) == i, total[:, i * per:(i + 1) * per], picked
+        )
+    rt_ref[...] = picked[:NE]
+    gn_ref[...] = picked[NE:NE + 1]
 
     for kind, out in enumerate((act_ref, igr_ref)):
         for m in range(NM):
@@ -462,7 +489,7 @@
         wait(ebs.at[kind], e_s.at[kind])
         p, r = ((ps_f, rf), (ps_b, rb))[kind]
         sends = me_l < NP - 1 if kind == 0 else me_l > 0
-        origin = me_l == 0 if kind == 0 else last == 1
+        origin = me_l == NP - 1 - kind
         for m in range(NM):
             wait(actb.at[kind, 0, m, 0], ac_s.at[kind, m])
             for s in range(2):
@@ -476,7 +503,7 @@
 
                 @pl.when(origin)
                 def _():
-                    wait(xall.at[kind, m, s, 0, pl.ds(0, 16 * NZ - 16)], ag0_s.at[kind, m, s])
+                    wait(xall.at[kind, m, s, 0], ag0_s.at[kind, m, s])
 
     wait(pmall.at[pl.ds(0, NE - 1)], m_s)
     for m in range(NM):
@@ -515,17 +542,18 @@
     sem = pltpu.SemaphoreType.DMA
     unit = sem((2, NM, 2))
     shape = jax.ShapeDtypeStruct
-    act, igr, gg, ug, dg, rg = pl.pallas_call(
+    per = DS // NE
+    results = pl.pallas_call(
         functools.partial(kernel, (NM, D, F, NE, ND, NP)),
         name="moe_layers",
         in_specs=[V, V, V, V, V, A, A, A],
-        out_specs=[V] * 6,
+        out_specs=[V] * 7,
         out_shape=[
             shape((NM, 8, D), BF), shape((NM, 8, D), BF), shape((DS, F), BF), shape((DS, F), BF),
-            shape((F, DS), BF), shape((NE + 8, 128), F32),
+            shape((F, DS), BF), shape((NE, per), F32), shape((1, per), F32),
         ],
         scratch_shapes=[
-            vm(D, F), vm(D, F), vm(F, D),
+            vm(D, F), vm(D, F), vm(F, D), vm(F, D), vm(F, D), vm(D, F),
             vm(2, NM, 16, Q), vm(2, 2, NM, 16, Q),
             vf(NE, NM, 8, 128),
             vm(2, NM, 2, 2, NZ * 16, Q), vm(NM, 2, R, D), vm(NM, 2, R, D),
@@ -548,11 +576,17 @@
         embedded, out_grad, routing[0], norm_gain, router_weight[0].T,
         gate_weight[0, 0], up_weight[0, 0], down_weight[0, 0],
     )
-    per = DS // NE
-    part = lax.dynamic_slice_in_dim(rg, lax.axis_index("expert") * per % 128, per, 1)
+    act, igr, gg, ug, dg, rt, gn = pl.pallas_call(
+        hand_over,
+        name="hand_over",
+        in_specs=[A] * 7,
+        out_specs=[A] * 7,
+        out_shape=[shape(v.shape, v.dtype) for v in results],
+        scratch_shapes=[pltpu.VMEM(v.shape, v.dtype) for v in results] + [sem((2, 7))],
+        compiler_params=pltpu.CompilerParams(vmem_limit_bytes=58 * 2**20),
+    )(*results)
     return (
-        act[None], igr[None], gg[None, None], ug[None, None], dg[None, None],
-        part[:NE].T[None], part[NE][None],
+        act[None], igr[None], gg[None, None], ug[None, None], dg[None, None], rt.T[None], gn,
     )
 
 

time: 246 us -> 226 us (0.919)
  local copies, waits for them, and re-layouts: 10.8 us -> 0 us
  Pallas kernels: 234 us -> 226 us
    pallas_call x1, Pallas kernels: 234 us -> 223 us  [local(): pl.pallas_call(functools.partial(kernel, (NM, D, F, NE, ND, NP)), name='m...]
    unnamed x7 -> x0, local copies, waits for them, and re-layouts: 8.08 us -> none
    pallas_call x0 -> x1, Pallas kernels: none -> 2.77 us  [local(): pl.pallas_call(hand_over, name='hand_over', in_specs=[A] * 7, out_specs=[...]
where the time goes in v4:
time: 226 us
  Pallas kernels  226 us (100%)
    pallas_call x1, Pallas kernels, local(): pl.pallas_call(functools.partial(kernel, (NM, D, F, NE, ND, NP)), name='m...  223 us

profile of v4, /device:TPU:1, one launch (start us, length us, event | category | flops | bytes accessed | tf_op | source)
XLA Modules:
  0.0 226.2 jit_solution(11252137576110856647)
XLA Ops:
  0.6 222.8 %moe_layers.1 = (bf16[3,8,2048]{2,1,0:T(8,128)(2,1)}, bf16[3,8,2048]{2,1,0:T(8,128)(2,1)}, bf16[512,768]{1,0:T(8,128)(2,1)}, bf16[512,768]{1,0:T(8,128)(2,1)}, b...) custom-call(bf16[3,8,2048]{2,1,0:T(8,128)(2,1)} %emb_ref.1, bf16[3,8,2048]{2,1,0:T(8,128)(2,1)} %og_ref.1, ...), custom_call_target="tpu_custom_call" | custom-call | tf_op jit(solution)/shard_map/moe_layers/pallas_call | solution.py:546
  223.4 2.8 %hand_over.1 = (bf16[3,8,2048]{2,1,0:T(8,128)(2,1)}, bf16[3,8,2048]{2,1,0:T(8,128)(2,1)}, bf16[512,768]{1,0:T(8,128)(2,1)}, bf16[512,768]{1,0:T(8,128)(2,1)}, bf...) custom-call(bf16[3,8,2048]{2,1,0:T(8,128)(2,1)} %get-tuple-element.21.refs_0_, ...), custom_call_target="tpu_custom_call" | custom-call | tf_op jit(solution)/shard_map/hand_over/pallas_call | solution.py:579

commit v5 on v4

--- a/solution.py
+++ b/solution.py
@@ -55,7 +55,7 @@
     ps_f, pr_f, ps_b, pr_b, qo_f, qo_b, qf, qb, rf, rb, actb,
     nsl, gsl, hid, dgu, racc, rgs, ybuf, ysum, zbuf,
     w_sem, e_s, e_r, m_s, m_r, ag0_s, ag_s, ag_r, fw_s, fw_r, pr_s, pr_rs, rs_s, rs_r, ac_s, ac_r,
-    y_s, y_r, yd_s, yd_r, yf_s, yf_r, r1_s, r1_r, r2_s, r2_r,
+    y_s, y_r, yd_s, yd_r, yf_s, yf_r, yl_r, yp_s, yp_r, r1_s, r1_r, r2_s, r2_r,
 ):
     NM, D, F, NE, ND, NP = sizes
     NZ, H, Q, R, DS = NE // 2, D // 2, D // 4, NE * 4, D // ND
@@ -299,16 +299,26 @@
         mine = dgu.at[me_y, m, s]
         send(mine, mine, yd_s.at[0, m, s], yd_r.at[0, m, s], {"dp": y_up})
         send(mine, mine, yd_s.at[1, m, s], yd_r.at[1, m, s], {"dp": y_down})
-        for j in range(1, ND):
-            yy = (me_y + j) % ND
-            send(part(gfull.at[m, s], yy), gsl.at[me_y, m, s], y_s.at[2, m], y_r.at[2, m], {"dp": yy})
-        copy(part(gfull.at[m, s], me_y), gsl.at[me_y, m, s], y_r.at[2, m])
+        copy(part(gfull.at[m, s], me_y), gsl.at[me_y, m, s], yl_r.at[m])
+
+        @pl.when(s == c)
+        def _():
+            for j in range(1, ND):
+                yy = (me_y + j) % ND
+                send(
+                    part(gfull.at[m, s], yy), gsl.at[me_y, m, s], y_s.at[2, m], y_r.at[2, m],
+                    {"dp": yy},
+                )
 
     def pass_on(m):
         for s, source, target in ((0, y_down, y_up), (1, y_up, y_down)):
             block = dgu.at[source, m, s]
             wait(block, yd_r.at[s, m, s])
             send(block, block, yf_s.at[m, s], yf_r.at[m, s], {"dp": target})
+        wait(gsl.at[pl.ds(0, ND - 1), m, 0], y_r.at[2, m])
+        for j in range(1, ND):
+            block = gsl.at[(me_y + j) % ND, m, c]
+            send(block, block, yp_s.at[m], yp_r.at[m], partner)
 
     def backward_result(m, s):
         wait(rb.at[m, s], rs_r.at[1, m, s])
@@ -378,14 +388,7 @@
         @pl.when(backward)
         def _():
             backward_compute(m, s)
-
-        @pl.when(forward & (u > 0))
-        def _():
-            forward_result(bm, bs)
-
-        @pl.when(backward & (u > 0))
-        def _():
-            backward_result(bm, bs)
+            backward_replicas(m, s)
 
         @pl.when(forward)
         def _():
@@ -395,7 +398,14 @@
         @pl.when(backward)
         def _():
             backward_scatter(m, s)
-            backward_replicas(m, s)
+
+        @pl.when(forward & (u > 0))
+        def _():
+            forward_result(bm, bs)
+
+        @pl.when(backward & (u > 0))
+        def _():
+            backward_result(bm, bs)
 
         @pl.when(backward & (s == 1) & (m > 0))
         def _():
@@ -436,7 +446,8 @@
     for m in range(NM):
         wait(hid.at[pl.ds(0, ND - 1), m], y_r.at[0, m])
         wait(nsl.at[:, m], y_r.at[1, m])
-        wait(gsl.at[:, m], y_r.at[2, m])
+        wait(gsl.at[0, m], yl_r.at[m])
+        wait(gsl.at[pl.ds(0, ND - 1), m, 0], yp_r.at[m])
     dg_ref[...] = dot(hid[...].reshape(rows, F), gsl[...].reshape(rows, DS), TN).astype(BF)
 
     per = DS // NE
@@ -507,8 +518,10 @@
 
     wait(pmall.at[pl.ds(0, NE - 1)], m_s)
     for m in range(NM):
-        for i, ref in enumerate((hid, nsl, gsl)):
+        for i, ref in enumerate((hid, nsl)):
             wait(ref.at[pl.ds(0, ND - 1), m], y_s.at[i, m])
+        wait(gsl.at[pl.ds(0, ND - 1), m, 0], y_s.at[2, m])
+        wait(gsl.at[pl.ds(0, ND - 1), m, 0], yp_s.at[m])
         for s in range(2):
             wait(dgu.at[0, m, s], yd_s.at[0, m, s])
             wait(dgu.at[0, m, s], yd_s.at[1, m, s])
@@ -566,7 +579,7 @@
             vf(NE + 8, H), vf(NE + 8, H), vf(ND, NE + 8, DS), vf(NE + 8, DS), vf(NZ, NE + 8, 128),
             sem((3,)), sem((2,)), sem((2,)), sem, sem,
             unit, unit, unit, unit, unit, unit, unit, unit, unit, sem((2, NM)), sem((2, NM)),
-            sem((3, NM)), sem((3, NM)), unit, unit, sem((NM, 2)), sem((NM, 2)),
+            sem((3, NM)), sem((3, NM)), unit, unit, sem((NM, 2)), sem((NM, 2)), sem((NM,)), sem((NM,)), sem((NM,)),
             sem((ND // 2,)), sem, sem, sem,
         ],
         compiler_params=pltpu.CompilerParams(

time: 226 us -> 208 us (0.920)
  Pallas kernels: 226 us -> 207 us
    pallas_call x1, Pallas kernels: 223 us -> 205 us  [local(): pl.pallas_call(functools.partial(kernel, (NM, D, F, NE, ND, NP)), name='m...]
where the time goes in v5:
time: 208 us
  Pallas kernels  207 us (100%)
    pallas_call x1, Pallas kernels, local(): pl.pallas_call(functools.partial(kernel, (NM, D, F, NE, ND, NP)), name='m...  205 us

profile of v5, /device:TPU:1, one launch (start us, length us, event | category | flops | bytes accessed | tf_op | source)
XLA Modules:
  0.0 208.1 jit_solution(17551957697373794761)
XLA Ops:
  0.6 204.7 %moe_layers.1 = (bf16[3,8,2048]{2,1,0:T(8,128)(2,1)}, bf16[3,8,2048]{2,1,0:T(8,128)(2,1)}, bf16[512,768]{1,0:T(8,128)(2,1)}, bf16[512,768]{1,0:T(8,128)(2,1)}, b...) custom-call(bf16[3,8,2048]{2,1,0:T(8,128)(2,1)} %emb_ref.1, bf16[3,8,2048]{2,1,0:T(8,128)(2,1)} %og_ref.1, ...), custom_call_target="tpu_custom_call" | custom-call | tf_op jit(solution)/shard_map/moe_layers/pallas_call | solution.py:559
  205.3 2.8 %hand_over.1 = (bf16[3,8,2048]{2,1,0:T(8,128)(2,1)}, bf16[3,8,2048]{2,1,0:T(8,128)(2,1)}, bf16[512,768]{1,0:T(8,128)(2,1)}, bf16[512,768]{1,0:T(8,128)(2,1)}, bf...) custom-call(bf16[3,8,2048]{2,1,0:T(8,128)(2,1)} %get-tuple-element.21.refs_0_, ...), custom_call_target="tpu_custom_call" | custom-call | tf_op jit(solution)/shard_map/hand_over/pallas_call | solution.py:592

commit v6 on v5

--- a/solution.py
+++ b/solution.py
@@ -393,20 +393,23 @@
         @pl.when(forward)
         def _():
             forward_scatter(m, s)
+
+        @pl.when(backward)
+        def _():
+            backward_scatter(m, s)
+
+        @pl.when(forward & (u > 0))
+        def _():
+            forward_result(bm, bs)
+
+        @pl.when(backward & (u > 0))
+        def _():
+            backward_result(bm, bs)
+
+        @pl.when(forward)
+        def _():
             forward_replicas(m, s)
 
-        @pl.when(backward)
-        def _():
-            backward_scatter(m, s)
-
-        @pl.when(forward & (u > 0))
-        def _():
-            forward_result(bm, bs)
-
-        @pl.when(backward & (u > 0))
-        def _():
-            backward_result(bm, bs)
-
         @pl.when(backward & (s == 1) & (m > 0))
         def _():
             pass_on(m - 1)
@@ -422,7 +425,6 @@
         return carry
 
     lax.fori_loop(0, 2 * units, step, 0)
-    pass_on(NM - 1)
 
     rgs[0:NE] = racc[0:NE]
     rgs[NE:NE + 8] = jnp.broadcast_to(
@@ -441,15 +443,7 @@
         def _():
             copy(src, ybuf.at[me_y], r1_r)
 
-    far = (me_y + 2) % ND
-    rows = ND * NM * 2 * R
-    for m in range(NM):
-        wait(hid.at[pl.ds(0, ND - 1), m], y_r.at[0, m])
-        wait(nsl.at[:, m], y_r.at[1, m])
-        wait(gsl.at[0, m], yl_r.at[m])
-        wait(gsl.at[pl.ds(0, ND - 1), m, 0], yp_r.at[m])
-    dg_ref[...] = dot(hid[...].reshape(rows, F), gsl[...].reshape(rows, DS), TN).astype(BF)
-
+    pass_on(NM - 1)
     per = DS // NE
 
     @pl.when(mine)
@@ -467,6 +461,15 @@
                     copy(src, zbuf.at[z], r2_r)
                 else:
                     send(src, zbuf.at[z], r2_s, r2_r, {"expert": ee})
+
+    far = (me_y + 2) % ND
+    rows = ND * NM * 2 * R
+    for m in range(NM):
+        wait(hid.at[pl.ds(0, ND - 1), m], y_r.at[0, m])
+        wait(nsl.at[:, m], y_r.at[1, m])
+        wait(gsl.at[0, m], yl_r.at[m])
+        wait(gsl.at[pl.ds(0, ND - 1), m, 0], yp_r.at[m])
+    dg_ref[...] = dot(hid[...].reshape(rows, F), gsl[...].reshape(rows, DS), TN).astype(BF)
 
     for m in range(NM):
         for s in range(2):

time: 208 us -> 207 us (level)
  no operation moved by 1% of the time
where the time goes in v6:
time: 207 us
  Pallas kernels  206 us (100%)
    pallas_call x1, Pallas kernels, local(): pl.pallas_call(functools.partial(kernel, (NM, D, F, NE, ND, NP)), name='m...  204 us

profile of v6, /device:TPU:1, one launch (start us, length us, event | category | flops | bytes accessed | tf_op | source)
XLA Modules:
  0.0 207.0 jit_solution(16601647035225561172)
XLA Ops:
  0.6 203.6 %moe_layers.1 = (bf16[3,8,2048]{2,1,0:T(8,128)(2,1)}, bf16[3,8,2048]{2,1,0:T(8,128)(2,1)}, bf16[512,768]{1,0:T(8,128)(2,1)}, bf16[512,768]{1,0:T(8,128)(2,1)}, b...) custom-call(bf16[3,8,2048]{2,1,0:T(8,128)(2,1)} %emb_ref.1, bf16[3,8,2048]{2,1,0:T(8,128)(2,1)} %og_ref.1, ...), custom_call_target="tpu_custom_call" | custom-call | tf_op jit(solution)/shard_map/moe_layers/pallas_call | solution.py:562
  204.2 2.8 %hand_over.1 = (bf16[3,8,2048]{2,1,0:T(8,128)(2,1)}, bf16[3,8,2048]{2,1,0:T(8,128)(2,1)}, bf16[512,768]{1,0:T(8,128)(2,1)}, bf16[512,768]{1,0:T(8,128)(2,1)}, bf...) custom-call(bf16[3,8,2048]{2,1,0:T(8,128)(2,1)} %get-tuple-element.21.refs_0_, ...), custom_call_target="tpu_custom_call" | custom-call | tf_op jit(solution)/shard_map/hand_over/pallas_call | solution.py:595
